TPU v7x, 32 devices: a whole 2x2x4 slice. The times are simulated.
32 devices in a mesh: wide: 8 (over y, x, core), narrow: 4 (over z).
Axes of the slice: x: 2, y: 2, z: 4, core: 2. Of those that a mesh axis runs over, the one named last changes fastest.
Arguments:
- tokens: bfloat16 [10240, 1120], P(('wide', 'narrow')), may hold values from -6 to 6
- lengths: int32 [32], P(('wide', 'narrow')), may hold values from 1 to 320
- norm1_gain: bfloat16 [1120], P('narrow'), may hold values from 0.099609375 to 1.8984375
- norm1_bias: bfloat16 [1120], P('narrow'), may hold values from -3 to 3
- qkv_weight: bfloat16 [1120, 3360], P('narrow'), may hold values from -0.1875 to 0.1875
- query_bias: bfloat16 [1120], P('narrow'), may hold values from -3 to 3
- value_bias: bfloat16 [1120], P('narrow'), may hold values from -3 to 3
- out_weight: bfloat16 [1120, 1120], P('narrow'), may hold values from -1.5 to 1.5
- out_bias: bfloat16 [1120], P('narrow'), may hold values from -3 to 3
- norm2_gain: bfloat16 [1120], P('narrow'), may hold values from 0.099609375 to 1.8984375
- norm2_bias: bfloat16 [1120], P('narrow'), may hold values from -3 to 3
- up_weight: bfloat16 [1120, 4480], P('narrow'), may hold values from -0.1875 to 0.1875
- up_bias: bfloat16 [4480], P('narrow'), may hold values from -3 to 3
- down_weight: bfloat16 [4480, 1120], P('narrow'), may hold values from -0.09375 to 0.09375
- down_bias: bfloat16 [1120], P('narrow'), may hold values from -3 to 3
- cotangent: bfloat16 [10240, 1120], P(('wide', 'narrow')), may hold values from -6 to 6
Outputs:
- block_out: bfloat16 [10240, 1120], P(('wide', 'narrow'))
- input_grad: float32 [10240, 1120], P(('wide', 'narrow'))
- norm1_gain_grad: float32 [1120], P('narrow')
- norm1_bias_grad: float32 [1120], P('narrow')
- qkv_weight_grad: float32 [1120, 3360], P('narrow', 'wide')
- query_bias_grad: float32 [1120], P('narrow')
- value_bias_grad: float32 [1120], P('narrow')
- out_weight_grad: float32 [1120, 1120], P('narrow', 'wide')
- out_bias_grad: float32 [1120], P('narrow')
- norm2_gain_grad: float32 [1120], P('narrow')
- norm2_bias_grad: float32 [1120], P('narrow')
- up_weight_grad: float32 [1120, 4480], P('narrow', 'wide')
- up_bias_grad: float32 [4480], P('narrow')
- down_weight_grad: float32 [4480, 1120], P('narrow', 'wide')
- down_bias_grad: float32 [1120], P('narrow')
All inputs are finite; a program needn't handle non-finite values.
Results may differ from a plain program's by a relative error of at most 0.012.
Values may be sent and summed in bfloat16 or wider, within the bound.
No kernel may reach another device: no remote copies, remote signals or barrier semaphores. Data moves between devices by JAX's collectives and lax.ppermute only.
A program may use at most 256 MiB of HBM per device.

v0:
```python
import jax
import jax.numpy as jnp
from jax import lax
from jax.sharding import PartitionSpec as P

HEADS = 20


EPSILON = 1e-05
FILL = -1000000000.0


def scaled_norm(values, gain):
    center = values - jnp.mean(values, axis=-1, keepdims=True)
    spread = jnp.mean(center * center, axis=-1, keepdims=True)
    return center * lax.rsqrt(spread + EPSILON) * gain


def gelu_tanh(values):
    return jax.nn.gelu(values, approximate=True)


def plain_product(first, second):
    return jnp.dot(first, second, preferred_element_type=jnp.float32)


def left_product(first, second):
    return lax.dot_general(
        first, second, (((0,), (0,)), ((), ())), preferred_element_type=jnp.float32
    )


def right_product(first, second):
    return lax.dot_general(
        first, second, (((1,), (1,)), ((), ())), preferred_element_type=jnp.float32
    )


def shards(
    tokens,
    lengths,
    norm1_gain,
    norm1_bias,
    qkv_weight,
    query_bias,
    value_bias,
    out_weight,
    out_bias,
    norm2_gain,
    norm2_bias,
    up_weight,
    up_bias,
    down_weight,
    down_bias,
    cotangent,
):
    cell_count = lengths.shape[0]
    row_count = tokens.shape[0]
    seq_slots = row_count // cell_count
    model_width = qkv_weight.shape[1] // 3
    head_count = HEADS
    head_width = model_width // head_count
    score_scale = head_width ** (-0.5)
    shape_heads = (cell_count, seq_slots, head_count, head_width)
    attn_full = (
        lax.all_gather(norm1_gain, "narrow", axis=0, tiled=True),
        lax.all_gather(norm1_bias, "narrow", axis=0, tiled=True),
        lax.all_gather(qkv_weight, "narrow", axis=0, tiled=True),
        lax.all_gather(query_bias, "narrow", axis=0, tiled=True),
        lax.all_gather(value_bias, "narrow", axis=0, tiled=True),
        lax.all_gather(out_weight, "narrow", axis=0, tiled=True),
        lax.all_gather(out_bias, "narrow", axis=0, tiled=True),
    )
    mlp_full = (
        lax.all_gather(norm2_gain, "narrow", axis=0, tiled=True),
        lax.all_gather(norm2_bias, "narrow", axis=0, tiled=True),
        lax.all_gather(up_weight, "narrow", axis=0, tiled=True),
        lax.all_gather(up_bias, "narrow", axis=0, tiled=True),
        lax.all_gather(down_weight, "narrow", axis=0, tiled=True),
        lax.all_gather(down_bias, "narrow", axis=0, tiled=True),
    )
    gain_one = attn_full[0].astype(jnp.float32)
    shift_one = attn_full[1].astype(jnp.float32)
    qkv_full = attn_full[2]
    query_shift = attn_full[3].astype(jnp.float32)
    value_shift = attn_full[4].astype(jnp.float32)
    out_full = attn_full[5]
    out_shift = attn_full[6].astype(jnp.float32)
    gain_two = mlp_full[0].astype(jnp.float32)
    shift_two = mlp_full[1].astype(jnp.float32)
    up_full = mlp_full[2]
    up_shift = mlp_full[3].astype(jnp.float32)
    down_full = mlp_full[4]
    down_shift = mlp_full[5].astype(jnp.float32)
    inputs = tokens.astype(jnp.float32)
    normed_low = (scaled_norm(inputs, gain_one) + shift_one).astype(jnp.bfloat16)
    joined = plain_product(normed_low, qkv_full)
    queries = (joined[:, :model_width] + query_shift).astype(jnp.bfloat16).reshape(shape_heads)
    keys_low = joined[:, model_width : 2 * model_width].astype(jnp.bfloat16).reshape(shape_heads)
    values_low = (
        (joined[:, 2 * model_width :] + value_shift).astype(jnp.bfloat16).reshape(shape_heads)
    )
    positions = jnp.arange(seq_slots)
    allowed = (positions[None, None, :] <= positions[None, :, None]) & (
        positions[None, None, :] < lengths[:, None, None]
    )
    scores = (
        jnp.einsum("cqhd,ckhd->chqk", queries, keys_low, preferred_element_type=jnp.float32)
        * score_scale
    )
    scores = jnp.where(allowed[:, None], scores, FILL)
    attn_probs = jax.nn.softmax(scores, axis=-1)
    probs_low = attn_probs.astype(jnp.bfloat16)
    context = jnp.einsum(
        "chqk,ckhd->cqhd", probs_low, values_low, preferred_element_type=jnp.float32
    )
    context = context.reshape(row_count, model_width).astype(jnp.bfloat16)
    middle = inputs + plain_product(context, out_full) + out_shift
    normed_two_low = (scaled_norm(middle, gain_two) + shift_two).astype(jnp.bfloat16)
    hidden_pre = plain_product(normed_two_low, up_full) + up_shift
    activated, gelu_pull = jax.vjp(gelu_tanh, hidden_pre)
    activated_low = activated.astype(jnp.bfloat16)
    mlp_out = plain_product(activated_low, down_full) + down_shift
    keep_rows = (positions[None, :] < lengths[:, None]).astype(jnp.float32).reshape(row_count, 1)
    block_out = (keep_rows * (middle + mlp_out)).astype(jnp.bfloat16)
    mlp_again = (
        lax.all_gather(norm2_gain, "narrow", axis=0, tiled=True),
        lax.all_gather(up_weight, "narrow", axis=0, tiled=True),
        lax.all_gather(down_weight, "narrow", axis=0, tiled=True),
    )
    attn_again = (
        lax.all_gather(norm1_gain, "narrow", axis=0, tiled=True),
        lax.all_gather(qkv_weight, "narrow", axis=0, tiled=True),
        lax.all_gather(out_weight, "narrow", axis=0, tiled=True),
    )
    gain_two_back = mlp_again[0].astype(jnp.float32)
    up_back = mlp_again[1]
    down_back = mlp_again[2]
    gain_one_back = attn_again[0].astype(jnp.float32)
    qkv_back = attn_again[1]
    out_back = attn_again[2]
    grad_rows = cotangent.astype(jnp.float32) * keep_rows
    grad_low = grad_rows.astype(jnp.bfloat16)
    down_shift_grad = jnp.sum(grad_rows, axis=0)
    act_grad = right_product(grad_low, down_back)
    pre_grad = gelu_pull(act_grad)[0].astype(jnp.bfloat16)
    up_shift_grad = jnp.sum(pre_grad.astype(jnp.float32), axis=0)
    two_grad = right_product(pre_grad, up_back)
    unused_two, norm_two_pull = jax.vjp(scaled_norm, middle, gain_two_back)
    middle_from_mlp, gain_two_grad = norm_two_pull(two_grad)
    shift_two_grad = jnp.sum(two_grad, axis=0)
    middle_grad = grad_rows + middle_from_mlp
    middle_low = middle_grad.astype(jnp.bfloat16)
    out_shift_grad = jnp.sum(middle_low.astype(jnp.float32), axis=0)
    context_grad = right_product(middle_low, out_back).astype(jnp.bfloat16).reshape(shape_heads)
    probs_grad = jnp.einsum(
        "cqhd,ckhd->chqk", context_grad, values_low, preferred_element_type=jnp.float32
    )
    value_grad = jnp.einsum(
        "chqk,cqhd->ckhd", probs_low, context_grad, preferred_element_type=jnp.float32
    )
    score_grad = attn_probs * (
        probs_grad - jnp.sum(attn_probs * probs_grad, axis=-1, keepdims=True)
    )
    score_low = score_grad.astype(jnp.bfloat16)
    query_grad = (
        jnp.einsum("chqk,ckhd->cqhd", score_low, keys_low, preferred_element_type=jnp.float32)
        * score_scale
    )
    key_grad = (
        jnp.einsum("chqk,cqhd->ckhd", score_low, queries, preferred_element_type=jnp.float32)
        * score_scale
    )
    joined_grad = jnp.concatenate(
        [
            query_grad.reshape(row_count, model_width),
            key_grad.reshape(row_count, model_width),
            value_grad.reshape(row_count, model_width),
        ],
        axis=1,
    ).astype(jnp.bfloat16)
    joined_sums = jnp.sum(joined_grad.astype(jnp.float32), axis=0)
    query_shift_grad = joined_sums[:model_width]
    value_shift_grad = joined_sums[2 * model_width :]
    one_grad = right_product(joined_grad, qkv_back)
    unused_one, norm_one_pull = jax.vjp(scaled_norm, inputs, gain_one_back)
    input_from_attn, gain_one_grad = norm_one_pull(one_grad)
    shift_one_grad = jnp.sum(one_grad, axis=0)
    input_grad = middle_grad + input_from_attn
    qkv_grad = left_product(normed_low, joined_grad)
    out_grad = left_product(context, middle_low)
    up_grad = left_product(normed_two_low, pre_grad)
    down_grad = left_product(activated_low, grad_low)
    every_shard = (
        lax.psum_scatter(gain_one_grad, "narrow", scatter_dimension=0, tiled=True),
        lax.psum_scatter(shift_one_grad, "narrow", scatter_dimension=0, tiled=True),
        lax.psum_scatter(qkv_grad, "narrow", scatter_dimension=0, tiled=True),
        lax.psum_scatter(query_shift_grad, "narrow", scatter_dimension=0, tiled=True),
        lax.psum_scatter(value_shift_grad, "narrow", scatter_dimension=0, tiled=True),
        lax.psum_scatter(out_grad, "narrow", scatter_dimension=0, tiled=True),
        lax.psum_scatter(out_shift_grad, "narrow", scatter_dimension=0, tiled=True),
        lax.psum_scatter(gain_two_grad, "narrow", scatter_dimension=0, tiled=True),
        lax.psum_scatter(shift_two_grad, "narrow", scatter_dimension=0, tiled=True),
        lax.psum_scatter(up_grad, "narrow", scatter_dimension=0, tiled=True),
        lax.psum_scatter(up_shift_grad, "narrow", scatter_dimension=0, tiled=True),
        lax.psum_scatter(down_grad, "narrow", scatter_dimension=0, tiled=True),
        lax.psum_scatter(down_shift_grad, "narrow", scatter_dimension=0, tiled=True),
    )
    (
        gain_one_piece,
        shift_one_piece,
        qkv_piece,
        query_piece,
        value_piece,
        out_piece,
        out_shift_piece,
        gain_two_piece,
        shift_two_piece,
        up_piece,
        up_shift_piece,
        down_piece,
        down_shift_piece,
    ) = every_shard
    vector_sums = lax.psum(
        (
            gain_one_piece,
            shift_one_piece,
            query_piece,
            value_piece,
            out_shift_piece,
            gain_two_piece,
            shift_two_piece,
            up_shift_piece,
            down_shift_piece,
        ),
        "wide",
    )
    matrix_sums = (
        lax.psum_scatter(qkv_piece, "wide", scatter_dimension=1, tiled=True),
        lax.psum_scatter(out_piece, "wide", scatter_dimension=1, tiled=True),
        lax.psum_scatter(up_piece, "wide", scatter_dimension=1, tiled=True),
        lax.psum_scatter(down_piece, "wide", scatter_dimension=1, tiled=True),
    )
    return (
        block_out,
        input_grad,
        vector_sums[0],
        vector_sums[1],
        matrix_sums[0],
        vector_sums[2],
        vector_sums[3],
        matrix_sums[1],
        vector_sums[4],
        vector_sums[5],
        vector_sums[6],
        matrix_sums[2],
        vector_sums[7],
        matrix_sums[3],
        vector_sums[8],
    )


def solution(mesh):
    placed = (
        P(("wide", "narrow"), None),
        P(("wide", "narrow")),
        P("narrow"),
        P("narrow"),
        P("narrow", None),
        P("narrow"),
        P("narrow"),
        P("narrow", None),
        P("narrow"),
        P("narrow"),
        P("narrow"),
        P("narrow", None),
        P("narrow"),
        P("narrow", None),
        P("narrow"),
        P(("wide", "narrow"), None),
    )
    return jax.shard_map(
        shards,
        mesh=mesh,
        in_specs=placed,
        out_specs=(
            P(("wide", "narrow"), None),
            P(("wide", "narrow"), None),
            P("narrow"),
            P("narrow"),
            P("narrow", "wide"),
            P("narrow"),
            P("narrow"),
            P("narrow", "wide"),
            P("narrow"),
            P("narrow"),
            P("narrow"),
            P("narrow", "wide"),
            P("narrow"),
            P("narrow", "wide"),
            P("narrow"),
        ),
        check_vma=False,
    )
```

profile of v0, /device:TPU:0, one launch (start us, length us, event | category | flops | bytes accessed | tf_op | source)
XLA Modules:
  0.0 1887.3 jit_solution(9406241276578316329)
XLA Ops:
  14.4 26.6 %all-reduce.27 = (bf16[1120]{0:T(1024)(128)(2,1)S(1)}, bf16[1120]{0:T(1024)(128)(2,1)S(1)}, bf16[1120]{0:T(1024)(128)(2,1)S(1)}, bf16[1120]{0:T(1024)(128)(2,1)S...) all-reduce(bf16[1120]{0:T(1024)(128)(2,1)S(1)} %dynamic-update-slic, ...), channel_id=1, replica_groups=mesh['wide'=8,'narrow'=4] {'narrow'}, use_global_device_ids=true, to_apply=%add.1 | all-reduce | flops 13440 | bytes 53760
  42.5 109.9 %all-gather.5.cloned.1.call-done = bf16[1120,3360]{1,0:T(8,128)(2,1)} async-done(((bf16[280,3360]{1,0:T(8,128)(2,1)}), bf16[1120,3360]{1,0:T(8,128)(2,1)}) %all-gather.5.cloned.1.call-update) | async-done | bytes 7526416 | tf_op jit(solution)/shard_map/all_gather | solution.py:68
  152.4 5.8 fusion.58
  165.3 5.9 fusion.68
  171.2 5.1 fusion.35
  176.3 30.1 %all-gather.7.cloned.1.call-done = bf16[1120,1120]{1,0:T(8,128)(2,1)} async-done(((bf16[280,1120]{1,0:T(8,128)(2,1)}), bf16[1120,1120]{1,0:T(8,128)(2,1)}) %all-gather.7.cloned.1.call-update) | async-done | bytes 2508816 | tf_op jit(solution)/shard_map/all_gather | solution.py:71
  206.5 3.1 fusion.69
  209.9 173.5 %all-gather.9.cloned.1.call-done = bf16[1120,4480]{1,0:T(8,128)(2,1)} async-done(((bf16[280,4480]{1,0:T(8,128)(2,1)}), bf16[1120,4480]{1,0:T(8,128)(2,1)}) %all-gather.9.cloned.1.call-update) | async-done | bytes 10035216 | tf_op jit(solution)/shard_map/all_gather | solution.py:77
  383.4 9.9 convolution_add_fusion
  393.3 171.0 %all-gather.11.cloned.1.call-done = bf16[4480,1120]{1,0:T(8,128)(2,1)} async-done(((bf16[1120,1120]{1,0:T(8,128)(2,1)}), bf16[4480,1120]{1,0:T(8,128)(2,1)}) %all-gather.11.cloned.1.call-update) | async-done | bytes 10035216 | tf_op jit(solution)/shard_map/all_gather | solution.py:79
  564.3 10.5 convert_reduce_fusion
  574.9 4.2 multiply_reduce_fusion.1
  581.9 3.9 fusion.70
  586.9 3.8 convolution_convert_fusion
  593.3 9.7 multiply_reduce_fusion
  603.0 11.0 multiply_convert_fusion
  614.0 4.5 multiply_convert_fusion.2
  619.6 5.7 fusion.38
  626.3 10.6 fusion.56
  637.0 13.0 fusion.45
  650.0 11.6 fusion.62
  661.6 15.1 reduce-scatter.23.cloned.1.call-done
  676.8 261.9 %reduce-scatter.21.cloned.1.call-done = f32[280,3360]{1,0:T(8,128)} async-done(((f32[1120,3360]{1,0:T(8,128)}), f32[280,3360]{1,0:T(8,128)}) %reduce-scatter.21.cloned.1.call-update) | async-done | bytes 3763216
  938.7 345.9 %reduce-scatter.17.cloned.1.call-done = f32[1120,1120]{1,0:T(8,128)} async-done(((f32[4480,1120]{1,0:T(8,128)}), f32[1120,1120]{1,0:T(8,128)}) %reduce-scatter.17.cloned.1.call-update) | async-done | bytes 5017616 | tf_op jit(solution)/shard_map/reduce_scatter | solution.py:206
  1284.6 371.9 %reduce-scatter.25.cloned.1.call-done = f32[280,4480]{1,0:T(8,128)} async-done(((f32[1120,4480]{1,0:T(8,128)}), f32[280,4480]{1,0:T(8,128)}) %reduce-scatter.25.cloned.1.call-update) | async-done | bytes 5017616
  1656.5 6.6 copy.73
  1669.2 7.2 fusion.63
  1679.9 21.7 %all-reduce.26 = (f32[1120]{0:T(1024)S(1)}, f32[1120]{0:T(1024)S(1)}, f32[1120]{0:T(1024)S(1)}, f32[1120]{0:T(1024)S(1)}, f32[1120]{0:T(1024)S(1)}, /*index=5*/f...) all-reduce(f32[1120]{0:T(1024)S(1)} %get-tuple-element.62, ...), channel_id=2, replica_groups=mesh['wide'=8,'narrow'=4] {'narrow'}, use_global_device_ids=true, to_apply=%region_12.13.clone | all-reduce | flops 13440 | bytes 107520
  1702.3 23.8 %all-reduce.24 = (f32[280]{0:T(512)}, f32[280]{0:T(512)}, f32[280]{0:T(512)}, f32[280]{0:T(512)}, f32[280]{0:T(512)}, /*index=5*/f32[280]{0:T(512)}, f32[280]{0:T(512)}, f32[1120]{0:T(1024)}, f32[280]{0:T(512)}) all-reduce(f32[280]{0:T(512)S(1)} %dynamic-slice.10, ...), channel_id=1, replica_groups=mesh['wide'=8,'narrow'=4] {'wide'}, use_global_device_ids=true, to_apply=%region_13.14 | all-reduce | flops 3360 | bytes 26880 | tf_op jit(solution)/shard_map/psum | solution.py:224
  1726.1 11.5 fusion.15
  1737.6 72.4 %all-reduce.30.cloned.1.call-done = (f32[280,3360]{1,0:T(8,128)}, f32[280,1120]{1,0:T(8,128)}, f32[1120,1120]{1,0:T(8,128)}) async-done(((f32[280,3360]{1,0:T(8,128)}, f32[280,1120]{1,0:T(8,128)}, f32[1120,1120]{1,0:T(8,128)}), (f32[280,3360]{1,0:T(8,128)}, f32[280,1120]{1,0:T(8,128)}, f32[1120,1120]{1,0:T(8,128)})) %all-reduce.30.cloned.1.call-update) | async-done | bytes 10035216
  1817.1 60.8 %reduce-scatter.19.cloned.1.call-done = f32[560,280]{1,0:T(8,128)} async-done(((f32[4480,280]{1,0:T(8,128)}), f32[560,280]{1,0:T(8,128)}) %reduce-scatter.19.cloned.1.call-update) | async-done | bytes 627216
  (161 shorter events, 39.6 us)
Async XLA Ops:
  7.2 145.2 %all-gather.5.cloned.1.call-start = ((), (), s32[]{:S(2)}) async-start(), calls=%async_computation.5 | async-start | bytes 9676800 | tf_op jit(solution)/shard_map/all_gather | solution.py:68
  7.9 198.6 %all-gather.7.cloned.1.call-start = ((), (), s32[]{:S(2)}) async-start(), calls=%async_computation.6 | async-start | bytes 3225600 | tf_op jit(solution)/shard_map/all_gather | solution.py:71
  8.7 3.4 copy-start.25
  8.7 3.6 copy-start.26
  8.7 3.9 copy-start.27
  8.7 4.1 copy-start.28
  8.7 4.4 copy-start.29
  8.7 4.6 copy-start.30
  8.7 4.9 copy-start.31
  8.8 5.1 copy-start.32
  8.8 5.3 copy-start.23
  8.8 33.0 %copy-start.1 = (bf16[320,1120]{1,0:T(8,128)(2,1)S(1)}, bf16[320,1120]{1,0:T(8,128)(2,1)}, u32[]{:S(2)}) copy-start(bf16[320,1120]{1,0:T(8,128)(2,1)} %param.16) | copy-start | bytes 2150404
  8.8 374.6 %all-gather.9.cloned.1.call-start = ((), (), s32[]{:S(2)}) async-start(), calls=%async_computation.7 | async-start | bytes 12544000 | tf_op jit(solution)/shard_map/all_gather | solution.py:77
  9.5 554.8 %all-gather.11.cloned.1.call-start = ((), (), s32[]{:S(2)}) async-start(), calls=%async_computation.8 | async-start | bytes 12902400 | tf_op jit(solution)/shard_map/all_gather | solution.py:79
  10.1 666.7 %reduce-scatter.23.cloned.1.call-start = ((), (), s32[]{:S(2)}) async-start(), calls=%async_computation.12 | async-start | bytes 6451200
  42.4 115.9 %copy-start.20 = (f32[320]{0:T(512)}, f32[320]{0:T(512)S(1)}, u32[]{:S(2)}) copy-start(f32[320]{0:T(512)S(1)} %fusion.29) | copy-start | bytes 3844
  162.6 8.6 copy-start.10
  165.3 5.9 copy-start.11
  176.3 33.3 %copy-start.8 = (bf16[20,56,320]{2,1,0:T(8,128)(2,1)}, bf16[20,56,320]{2,1,0:T(8,128)(2,1)S(1)}, u32[]{:S(2)}) copy-start(bf16[20,56,320]{2,1,0:T(8,128)(2,1)S(1)} %fusion.35) | copy-start | bytes 2150404
  209.9 354.4 %copy-start.6 = (bf16[320,1120]{1,0:T(8,128)(2,1)S(1)}, bf16[320,1120]{1,0:T(8,128)(2,1)}, u32[]{:S(2)}) copy-start(bf16[320,1120]{1,0:T(8,128)(2,1)} %param.31) | copy-start | bytes 2150404
  564.3 10.6 copy-start.33
  574.9 4.2 copy-start.17
  585.8 352.9 %reduce-scatter.21.cloned.1.call-start = ((), (), s32[]{:S(2)}) async-start(), calls=%async_computation.11 | async-start | bytes 19353600
  593.3 9.7 copy-start.18
  614.0 4.5 copy-start
  614.0 4.5 copy-start.12
  619.6 5.7 copy-start.4
  636.9 647.6 %reduce-scatter.17.cloned.1.call-start = ((), (), s32[]{:S(2)}) async-start(), calls=%async_computation.9 | async-start | bytes 25804800 | tf_op jit(solution)/shard_map/reduce_scatter | solution.py:206
  650.0 1006.6 %reduce-scatter.25.cloned.1.call-start = ((), (), s32[]{:S(2)}) async-start(), calls=%async_computation.13 | async-start | bytes 25088000
  661.6 1148.4 %all-reduce.30.cloned.1.call-start = ((), (), s32[]{:S(2)}) async-start(), calls=%async_computation.14 | async-start | bytes 20643840
  1284.6 593.3 %reduce-scatter.19.cloned.1.call-start = ((), (), s32[]{:S(2)}) async-start(), calls=%async_computation.10 | async-start | bytes 7741440
  1669.2 7.2 copy-start.21
  (13 other events, 19.1 us)
Sparse Core Ops, SparseCore 0:
  9.6 142.7 all-gather.4
  154.0 52.4 all-gather.6
  208.0 175.3 all-gather.8
  384.8 179.4 all-gather.10
  586.0 90.7 reduce-scatter.22
  679.1 259.5 reduce-scatter.20
  941.1 343.4 reduce-scatter.16
  1287.0 369.4 reduce-scatter.24
  1661.1 148.7 all-reduce.29
  1813.3 64.5 reduce-scatter.18
where the time goes:
time: 1890 us
  waiting for transfers between devices  1620 us (86%)
  matrix products  127 us (7%)
  blocking collectives  72.1 us (4%)
  local copies, waits for them, and re-layouts  34.8 us (2%)
  between operations  19.6 us (1%)
    unnamed x15, waiting for transfers between devices  785 us
    reduce_scatter x1, waiting for transfers between devices, shards(): lax.psum_scatter(down_grad, 'narrow', scatter_dimension=0, tiled=True)  346 us
    all_gather x1, waiting for transfers between devices, shards(): lax.all_gather(up_weight, 'narrow', axis=0, tiled=True)  173 us
    all_gather x1, waiting for transfers between devices, shards(): lax.all_gather(down_weight, 'narrow', axis=0, tiled=True)  171 us
    all_gather x1, waiting for transfers between devices, shards(): lax.all_gather(qkv_weight, 'narrow', axis=0, tiled=True)  110 us
    unnamed x2, blocking collectives  48.3 us
    dot_general x4, matrix products, left_product(): lax.dot_general(first, second, (((0,), (0,)), ((), ())), preferred_elemen...  39 us
  transfers between devices with their start and end apart: 10, of which 10 were waited for; matrix products, arithmetic and copies ran while one was open for 8% of the time, Pallas kernels for 0%

commit v1 on v0

v1 whole, which is shorter than its diff:
```python
import jax
import jax.numpy as jnp
from jax import lax
from jax.sharding import Mesh, PartitionSpec as P

HEADS = 20
EPSILON = 1e-05
FILL = -1000000000.0
BF = jnp.bfloat16
F32 = jnp.float32
AXES = ("o", "y", "x", "c", "z")
WIDE = ("o", "y", "x", "c")
SWAP = [(0, 1), (1, 0)]
GROUP = 4


def swap(value, axis):
    return lax.ppermute(value, axis, SWAP)


def dot(first, second):
    return jnp.dot(first, second, preferred_element_type=F32)


def dot_left(first, second):
    return lax.dot_general(first, second, (((0,), (0,)), ((), ())), preferred_element_type=F32)


def dot_right(first, second):
    return lax.dot_general(first, second, (((1,), (1,)), ((), ())), preferred_element_type=F32)


def pick(blocks, index):
    return lax.dynamic_index_in_dim(blocks, index, 0, keepdims=False)


def choose(flag, first, second):
    return jnp.where(flag == 0, first, second)


def group_gather(value):
    over_core = swap(value, "c")
    over_x = swap(value, "x")
    return [value, over_core, over_x, swap(over_x, "c")]


def group_scatter(parts):
    sent = swap(jnp.stack([parts[1], parts[3]]).astype(BF), "c")
    ours = parts[0] + sent[0].astype(F32)
    theirs = (parts[2] + sent[1].astype(F32)).astype(BF)
    return ours + swap(theirs, "x").astype(F32)


def group_exchange(parts):
    far = swap(jnp.stack([parts[2], parts[3]]), "x")
    near = swap(jnp.stack([parts[1], far[1]]), "c")
    return [parts[0], near[0], far[0], near[1]]


def depth_shift(value, shift, count):
    return lax.ppermute(value, "z", [(i, (i + shift) % count) for i in range(count)])


def depth_place(blocks, here, count):
    return jnp.stack([pick(blocks, (here - z) % count) for z in range(count)])


def depth_scatter(parts, here, count):
    total = pick(parts, here).astype(F32)
    for shift in range(1, count):
        total = total + depth_shift(pick(parts, (here + shift) % count), shift, count).astype(F32)
    return total


def normal(values):
    center = values - jnp.mean(values, axis=-1, keepdims=True)
    spread = jnp.mean(center * center, axis=-1, keepdims=True)
    inverse = lax.rsqrt(spread + EPSILON)
    return center * inverse, inverse


def normal_back(grad, unit, inverse):
    return (
        grad
        - jnp.mean(grad, axis=-1, keepdims=True)
        - unit * jnp.mean(grad * unit, axis=-1, keepdims=True)
    ) * inverse


def gelu_tanh(values):
    return jax.nn.gelu(values, approximate=True)


def build(outer, depth):
    def shards(
        tokens, lengths, norm1_gain, norm1_bias, qkv_weight, query_bias, value_bias, out_weight,
        out_bias, norm2_gain, norm2_bias, up_weight, up_bias, down_weight, down_bias, cotangent,
    ):
        rows, width = tokens.shape
        cells = lengths.shape[0]
        slots = rows // cells
        hidden = up_weight.shape[1]
        heads = HEADS // GROUP
        head = width // HEADS
        part = width // GROUP
        part_depth = width // depth
        hidden_depth = hidden // depth
        block = hidden_depth // GROUP
        mine = depth * block
        wide = outer * 2 * GROUP
        scale = head ** (-0.5)
        y, x, c, z = (lax.axis_index(name) for name in ("y", "x", "c", "z"))
        member = 2 * x + c
        row = outer * 2

        vectors = jnp.concatenate(
            [norm1_gain, norm1_bias, query_bias, value_bias, out_bias, norm2_gain, norm2_bias, down_bias, up_bias]
        ).reshape(12, part_depth)
        vectors = depth_place(
            jnp.stack([vectors] + [depth_shift(vectors, r, depth) for r in range(1, depth)]), z, depth
        ).astype(F32)
        whole = jnp.transpose(vectors[:, :8], (1, 0, 2)).reshape(8, width)
        gain_one, shift_one, query_shift, value_shift, out_shift, gain_two, shift_two, down_shift = whole
        query_shift = pick(query_shift.reshape(GROUP, part), member)
        value_shift = pick(value_shift.reshape(GROUP, part), member)
        up_shift = lax.dynamic_slice_in_dim(
            vectors[:, 8:].reshape(depth, hidden_depth), member * block, block, 1
        ).reshape(mine)

        half = (part_depth // 2 + 7) // 8 * 8
        start = part_depth - half
        qkv_own = lax.dynamic_slice_in_dim(
            qkv_weight.reshape(part_depth, 3, width), member * part, part, 2
        ).reshape(part_depth, 3 * part)
        qkv_half = choose(y, qkv_own[:half], qkv_own[start:])
        near = jnp.stack([depth_shift(qkv_half, r, depth) for r in range(1, depth)])
        far = swap(near, "y")
        qkv_rest = jnp.concatenate(
            [choose(y, near, far), choose(y, far, near)[:, 2 * half - part_depth :]], axis=1
        )
        qkv_full = depth_place(jnp.concatenate([qkv_own[None], qkv_rest]), z, depth).reshape(width, 3 * part)

        inputs = tokens.astype(F32)
        unit_one, inverse_one = normal(inputs)
        normed_one = (unit_one * gain_one + shift_one).astype(BF)
        normed_one_all = jnp.concatenate(group_gather(normed_one))
        lengths_all = jnp.concatenate(group_gather(lengths))

        up_own = lax.dynamic_slice_in_dim(
            up_weight.reshape(part_depth, depth, hidden_depth), member * block, block, 2
        ).reshape(part_depth, mine)
        down_own = lax.dynamic_slice_in_dim(down_weight, member * block, block, 0)

        pieces = 2 * GROUP
        height = (part_depth // pieces + 7) // 8 * 8
        starts = [(p * (part_depth - height) // (pieces - 1)) // 8 * 8 for p in range(pieces - 1)] + [part_depth - height]
        ends = starts[1:] + [part_depth]
        place = 4 * y + member
        out_piece = lax.dynamic_slice_in_dim(out_weight, jnp.array(starts)[place], height, 0)
        got = jnp.stack([depth_shift(out_piece, r, depth) for r in range(1, depth)])[:, None]
        for axis, flag in (("c", c), ("x", x), ("y", y)):
            other = swap(got, axis)
            got = jnp.concatenate([choose(flag, got, other), choose(flag, other, got)], axis=1)
        out_rest = jnp.concatenate([got[:, p, : ends[p] - starts[p]] for p in range(pieces)], axis=1)
        out_full = depth_place(jnp.concatenate([out_weight[None], out_rest]), z, depth).reshape(width, width)

        turn = choose(y, up_own, down_own) if part_depth == block and mine == width else None
        if turn is None:
            up_rest = jnp.stack([depth_shift(up_own, r, depth) for r in range(1, depth)])
            down_rest = jnp.stack([depth_shift(down_own, r, depth) for r in range(1, depth)])
        else:
            near = jnp.stack([depth_shift(turn, r, depth) for r in range(1, depth)])
            far = swap(near, "y")
            up_rest, down_rest = choose(y, near, far), choose(y, far, near)
        up_full = depth_place(jnp.concatenate([up_own[None], up_rest]), z, depth).reshape(width, mine)
        down_full = depth_place(jnp.concatenate([down_own[None], down_rest]), z, depth).reshape(mine, width)

        positions = jnp.arange(slots)
        keep = (positions[None, :] < lengths[:, None]).astype(F32).reshape(rows, 1)
        grad_rows = cotangent.astype(F32) * keep
        grad_all = jnp.concatenate(group_gather(grad_rows.astype(BF)))

        joined = dot(normed_one_all, qkv_full)
        shape = (GROUP * cells, slots, heads, head)
        queries = (joined[:, :part] + query_shift).astype(BF).reshape(shape)
        keys = joined[:, part : 2 * part].astype(BF).reshape(shape)
        values = (joined[:, 2 * part :] + value_shift).astype(BF).reshape(shape)
        allowed = (positions[None, None, :] <= positions[None, :, None]) & (
            positions[None, None, :] < lengths_all[:, None, None]
        )
        scores = jnp.einsum("cqhd,ckhd->chqk", queries, keys, preferred_element_type=F32) * scale
        probs = jax.nn.softmax(jnp.where(allowed[:, None], scores, FILL), axis=-1)
        probs_low = probs.astype(BF)
        context = jnp.einsum("chqk,ckhd->cqhd", probs_low, values, preferred_element_type=F32)
        context = context.astype(BF).reshape(GROUP, rows, part)
        context = jnp.stack(group_exchange([context[k] for k in range(GROUP)]))
        context = jnp.concatenate([pick(context, member ^ k) for k in range(GROUP)], axis=1)

        middle = inputs + (dot(context, out_full) + out_shift)
        unit_two, inverse_two = normal(middle)
        normed_two = (unit_two * gain_two + shift_two).astype(BF)
        normed_two_all = jnp.concatenate(group_gather(normed_two))

        pre = dot(normed_two_all, up_full) + up_shift
        activated, gelu_pull = jax.vjp(gelu_tanh, pre)
        activated = activated.astype(BF)
        pre_grad = gelu_pull(dot_right(grad_all, down_full))[0].astype(BF)
        two_parts = dot_right(pre_grad, up_full).reshape(GROUP, rows, width)
        two_grad = group_scatter([two_parts[k] for k in range(GROUP)])
        mlp_parts = dot(activated, down_full).reshape(GROUP, rows, width)
        mlp_out = group_scatter([mlp_parts[k] for k in range(GROUP)]) + down_shift
        block_out = (keep * (middle + mlp_out)).astype(BF)

        middle_grad = grad_rows + normal_back(two_grad * gain_two, unit_two, inverse_two)
        middle_low = middle_grad.astype(BF)
        context_grad = dot_right(middle_low, out_full).astype(BF)
        context_grad = jnp.transpose(context_grad.reshape(rows, GROUP, part), (1, 0, 2))
        context_grad = group_exchange([pick(context_grad, member ^ k) for k in range(GROUP)])
        context_grad = jnp.stack(context_grad).reshape(shape)

        probs_grad = jnp.einsum("cqhd,ckhd->chqk", context_grad, values, preferred_element_type=F32)
        value_grad = jnp.einsum("chqk,cqhd->ckhd", probs_low, context_grad, preferred_element_type=F32)
        score_grad = probs * (probs_grad - jnp.sum(probs * probs_grad, axis=-1, keepdims=True))
        score_grad = score_grad.astype(BF)
        query_grad = jnp.einsum("chqk,ckhd->cqhd", score_grad, keys, preferred_element_type=F32) * scale
        key_grad = jnp.einsum("chqk,cqhd->ckhd", score_grad, queries, preferred_element_type=F32) * scale
        total = GROUP * rows
        joined_grad = jnp.concatenate(
            [query_grad.reshape(total, part), key_grad.reshape(total, part), value_grad.reshape(total, part)], axis=1
        ).astype(BF)
        one_parts = dot_right(joined_grad, qkv_full).reshape(GROUP, rows, width)
        one_grad = group_scatter([one_parts[k] for k in range(GROUP)])
        input_grad = middle_grad + normal_back(one_grad * gain_one, unit_one, inverse_one)

        each = mine // row
        side = width // row

        def columns(array, count, index):
            array = array.reshape(array.shape[0], outer, 2, count)
            return lax.dynamic_index_in_dim(array, index, 2, keepdims=False).reshape(array.shape[0], outer * count)

        def both(left, right, count):
            sent = swap(dot_left(left, columns(right, count, 1 - y)).astype(BF), "y")
            return (dot_left(left, columns(right, count, y)) + sent.astype(F32)).astype(BF)

        def over_outer(piece, count):
            piece = piece.reshape(piece.shape[0], outer, count)
            if outer == 1:
                return piece[:, 0]
            return lax.psum_scatter(piece, "o", scatter_dimension=1, tiled=False)

        down_piece = over_outer(
            depth_scatter(both(activated, grad_all, side).reshape(depth, block, outer * side), z, depth), side
        ).astype(BF)
        up_piece = over_outer(
            depth_scatter(both(normed_two_all, pre_grad, each).reshape(depth, part_depth, outer * each), z, depth), each
        ).astype(BF)
        down_all = jnp.stack(group_gather(down_piece))
        up_all = jnp.stack(group_gather(up_piece))
        down_all = jnp.stack([pick(down_all, member ^ k) for k in range(GROUP)])
        down_weight_grad = lax.dynamic_index_in_dim(
            down_all.reshape(hidden_depth, GROUP, side // GROUP), member, 1, keepdims=False
        ).astype(F32)
        up_all = up_all.reshape(GROUP, part_depth, each // block, block)
        ratio = wide // depth
        fold = GROUP // ratio
        up_pieces = []
        for k in range(fold):
            source = (member % ratio) * fold + k if fold > 1 else member
            chunk = pick(up_all, member ^ source)
            up_pieces.append(lax.dynamic_index_in_dim(chunk, member // ratio, 1, keepdims=False))
        up_weight_grad = jnp.concatenate(up_pieces, axis=1).astype(F32)

        out_parts = dot_left(middle_low, context).astype(BF).reshape(outer, 2, 2, 2, width // wide, width)
        for axis, flag in ((3, c), (2, x), (1, y)):
            sent = swap(lax.dynamic_index_in_dim(out_parts, 1 - flag, axis, keepdims=False), AXES[axis])
            out_parts = lax.dynamic_index_in_dim(out_parts, flag, axis, keepdims=False).astype(F32) + sent.astype(F32)
            out_parts = out_parts.astype(BF)
        out_parts = jnp.transpose(out_parts.reshape(outer, width // wide, depth, part_depth), (2, 0, 1, 3))
        out_piece = depth_scatter(out_parts, z, depth)
        out_piece = out_piece[0] if outer == 1 else lax.psum_scatter(out_piece, "o", scatter_dimension=0, tiled=False)
        out_weight_grad = out_piece.T

        qkv_parts = dot_left(normed_one_all, joined_grad).reshape(depth, part_depth, 3 * part)
        top, bottom = qkv_parts[:, :half], qkv_parts[:, start:]
        sent = swap(choose(y, bottom, top).astype(BF), "y")
        qkv_parts = (choose(y, top, bottom) + sent.astype(F32)).astype(BF)
        qkv_piece = depth_scatter(qkv_parts, z, depth).astype(BF)
        qkv_all = jnp.stack(group_gather(qkv_piece))
        qkv_all = jnp.stack([pick(qkv_all, member ^ k) for k in range(GROUP)]).reshape(GROUP, half, 3, part)
        qkv_all = jnp.transpose(qkv_all, (1, 2, 0, 3)).reshape(half, outer, 2, GROUP, 3 * width // wide)
        qkv_all = lax.dynamic_index_in_dim(qkv_all, member, 3, keepdims=False)
        if outer > 1:
            qkv_all = lax.psum_scatter(qkv_all, "o", scatter_dimension=1, tiled=True)
        qkv_all = qkv_all[:, 0]
        sent = swap(lax.dynamic_index_in_dim(qkv_all, 1 - y, 1, keepdims=False), "y")
        kept = lax.dynamic_index_in_dim(qkv_all, y, 1, keepdims=False)
        qkv_weight_grad = jnp.concatenate(
            [choose(y, kept, sent), choose(y, sent, kept)[2 * half - part_depth :]]
        ).astype(F32)

        def spread_out(vector):
            zero = jnp.zeros((GROUP,) + vector.shape, F32)
            return lax.dynamic_update_index_in_dim(zero, vector, member, 0)

        joined_sums = jnp.sum(joined_grad.astype(F32), axis=0)
        sums = [
            jnp.sum(one_grad * unit_one, axis=0),
            jnp.sum(one_grad, axis=0),
            spread_out(joined_sums[:part]).reshape(width),
            spread_out(joined_sums[2 * part :]).reshape(width),
            jnp.sum(middle_low.astype(F32), axis=0),
            jnp.sum(two_grad * unit_two, axis=0),
            jnp.sum(two_grad, axis=0),
            jnp.sum(grad_rows, axis=0),
        ]
        up_sums = spread_out(jnp.sum(pre_grad.astype(F32), axis=0).reshape(depth, block))
        up_sums = jnp.transpose(up_sums, (1, 0, 2)).reshape(depth, hidden_depth)
        packed = jnp.concatenate([total_of.reshape(depth, part_depth) for total_of in sums] + [up_sums], axis=1)
        packed = depth_scatter(packed, z, depth)
        for axis in ("c", "x", "y"):
            packed = packed + swap(packed, axis)
        if outer > 1:
            packed = lax.psum(packed, "o")
        vector = [packed[k * part_depth : (k + 1) * part_depth] for k in range(8)]
        return (
            block_out, input_grad, vector[0], vector[1], qkv_weight_grad, vector[2], vector[3], out_weight_grad,
            vector[4], vector[5], vector[6], up_weight_grad, packed[8 * part_depth :], down_weight_grad, vector[7],
        )

    return shards


def solution(mesh):
    wide, depth = mesh.shape["wide"], mesh.shape["narrow"]
    outer = wide // 8
    fine = Mesh(mesh.devices.reshape(outer, 2, 2, 2, depth), AXES)
    rows, vec, mat = P(AXES, None), P("z"), P("z", None)
    placed = (
        rows, P(AXES), vec, vec, mat, vec, vec, mat, vec, vec, vec, mat, vec, mat, vec, rows,
    )
    grad = P("z", WIDE)
    return jax.shard_map(
        build(outer, depth),
        mesh=fine,
        in_specs=placed,
        out_specs=(rows, rows, vec, vec, grad, vec, vec, grad, vec, vec, vec, grad, vec, grad, vec),
        check_vma=False,
    )
```

time: 1890 us -> 666 us (0.35)
  waiting for transfers between devices: 1620 us -> 256 us
  local copies, waits for them, and re-layouts: 34.8 us -> 131 us
  starting transfers between devices: 0.39 us -> 74.9 us
  other arithmetic: 18.2 us -> 91.7 us
  blocking collectives: 72.1 us -> 0 us
  matrix products: 127 us -> 96.7 us
    unnamed x15 -> x0, waiting for transfers between devices: 785 us -> none
    all_gather x4 -> x0, waiting for transfers between devices: 485 us -> none  [the longest x1 173 us: shards(): lax.all_gather(up_weight, 'narrow', axis=0, tiled=True)]
    reduce_scatter x1 -> x0, waiting for transfers between devices: 346 us -> none  [shards(): lax.psum_scatter(down_grad, 'narrow', scatter_dimension=0, tiled=True)]
    ppermute x0 -> x73, waiting for transfers between devices: none -> 256 us  [the longest x46 129 us: swap(): return lax.ppermute(value, axis, SWAP)]
    ppermute x0 -> x73, starting transfers between devices: none -> 74.9 us  [the longest x27 44.3 us: depth_shift(): lax.ppermute(value, 'z', [(i, (i + shift) % count) for i in range(count)])]
    unnamed x2 -> x0, blocking collectives: 48.3 us -> none
    reshape x0 -> x23, local copies, waits for them, and re-layouts: none -> 43.9 us  [the longest x1 6.4 us: shards(): up_weight.reshape(part_depth, depth, hidden_depth)]
    dot_general x16 -> x18, matrix products: 115 us -> 81.5 us  [the longest x6 23.9 us: dot_left(): lax.dot_general(first, second, (((0,), (0,)), ((), ())), preferred_elemen...]
  transfers between devices with their start and end apart: 10 -> 73, of which waited for: 10 -> 27; matrix products, arithmetic and copies ran while one was open for 8% -> 46% of each run, Pallas kernels for 0% -> 0%
where the time goes in v1:
time: 666 us; the launch traced here: 655 us
  waiting for transfers between devices  256 us (38%)
  local copies, waits for them, and re-layouts  131 us (20%)
  matrix products  96.7 us (15%)
  other arithmetic  91.7 us (14%)
  starting transfers between devices  74.9 us (11%)
    ppermute x46, waiting for transfers between devices, swap(): return lax.ppermute(value, axis, SWAP)  129 us
    ppermute x27, waiting for transfers between devices, depth_shift(): lax.ppermute(value, 'z', [(i, (i + shift) % count) for i in range(count)])  127 us
    ppermute x27, starting transfers between devices, depth_shift(): lax.ppermute(value, 'z', [(i, (i + shift) % count) for i in range(count)])  44.3 us
    ppermute x46, starting transfers between devices, swap(): return lax.ppermute(value, axis, SWAP)  30.6 us
    dot_general x6, matrix products, dot_left(): lax.dot_general(first, second, (((0,), (0,)), ((), ())), preferred_elemen...  23.9 us
    dot_general x4, matrix products, dot_right(): lax.dot_general(first, second, (((1,), (1,)), ((), ())), preferred_elemen...  23.4 us
    dot_general x4, matrix products, dot(): return jnp.dot(first, second, preferred_element_type=F32)  16.4 us
  transfers between devices with their start and end apart: 73, of which 27 were waited for; matrix products, arithmetic and copies ran while one was open for 46% of the time, Pallas kernels for 0%

profile of v1, /device:TPU:0, one launch (start us, length us, event | category | flops | bytes accessed | tf_op | source)
XLA Modules:
  0.0 655.4 jit_solution(2872130406457475373)
XLA Ops:
  3.7 6.3 concatenate.57
  19.3 6.4 reshape.422
  31.2 5.2 reshape.416
  78.7 4.8 collective-permute-done.7
  88.0 37.0 %collective-permute-done.6 = bf16[144,840]{1,0:T(8,128)(2,1)} collective-permute-done((bf16[144,840]{1,0:T(8,128)(2,1)}, bf16[144,840]{1,0:T(8,128)(2,1)}, u32[]{:S(2)}, u32[]{:S(2)}) %collective-permute-start.6) | collective-permute-done | bytes 241952 | tf_op jit(solution)/shard_map/ppermute | solution.py:61
  126.9 17.0 %collective-permute-done.25 = bf16[280,1120]{1,0:T(8,128)(2,1)S(1)} collective-permute-done((bf16[280,1120]{1,0:T(8,128)(2,1)}, bf16[280,1120]{1,0:T(8,128)(2,1)S(1)}, u32[]{:S(2)}, u32[]{:S(2)}) %collective-permute-start.25) | collective-permute-done | bytes 627232 | tf_op jit(solution)/shard_map/ppermute | solution.py:61
  150.6 11.9 %collective-permute-done.4 = bf16[320,1120]{1,0:T(8,128)(2,1)S(1)} collective-permute-done((bf16[320,1120]{1,0:T(8,128)(2,1)}, bf16[320,1120]{1,0:T(8,128)(2,1)S(1)}, u32[]{:S(2)}, u32[]{:S(2)}) %collective-permute-start.4) | collective-permute-done | bytes 716832 | tf_op jit(solution)/shard_map/ppermute | solution.py:18
  185.1 8.8 %fusion.157 = (f32[4,5,320]{2,1,0:T(8,128)S(1)}, f32[4,5,320,320]{2,3,1,0:T(8,128)}) fusion(pred[4,320,320]{1,2,0:T(8,128)(4,1)} %broadcast_and_fusion, bf16[4,320,5,56]{1,0,3,2:T(4,128)(2,1)} %reshape.420, bf16[4,320,5,56]{1,0,3,2:T(4,128)(2,1)S(1)} %reshape.419), kind=kOutput, calls=%fused_computation.364 | convolution fusion | flops 237568320 | bytes 10060800 | tf_op jit(solution)/shard_map/sub | solution.py:192
  193.9 5.1 fusion.68
  205.2 5.6 copy.196
  213.4 17.8 %collective-permute-done.20 = bf16[3,4,40,1120]{3,2,0,1:T(8,128)(2,1)} collective-permute-done((bf16[3,4,40,1120]{3,2,0,1:T(8,128)(2,1)}, bf16[3,4,40,1120]{3,2,0,1:T(8,128)(2,1)}, u32[]{:S(2)}, u32[]{:S(2)}) %collective-permute-start.20) | collective-permute-done | bytes 1075232 | tf_op jit(solution)/shard_map/ppermute | solution.py:18
  243.9 13.2 %collective-permute-done.22 = bf16[320,1120]{1,0:T(8,128)(2,1)S(1)} collective-permute-done((bf16[320,1120]{1,0:T(8,128)(2,1)S(1)}, bf16[320,1120]{1,0:T(8,128)(2,1)S(1)}, u32[]{:S(2)}, u32[]{:S(2)}) %collective-permute-start.22) | collective-permute-done | bytes 716832 | tf_op jit(solution)/shard_map/ppermute | solution.py:18
  259.3 5.5 multiply_convert_fusion.1
  269.5 6.2 fusion.168
  275.7 9.5 %convert_reduce_fusion = (f32[1120]{0:T(1024)S(1)}, bf16[1280,1120]{0,1:T(8,128)(2,1)S(1)}) fusion(f32[1280,1120]{0,1:T(8,128)S(1)} %get-tuple-element.148, bf16[1120,1120]{1,0:T(8,128)(2,1)S(1)} %bitcast.289, bf16[320,1120]{1,0:T(8,128)(2,1)} %collective-permute-done.32, bf16[320,1120]{1,0:T(8,128)(2,1)} %collective-permute-done.31, ...), kind=kOutput, calls=%fused_computation.17 | convolution fusion | flops 3254270976 | bytes 13982080 | tf_op jit(solution)/shard_map/dot_general | solution.py:30
  290.2 6.7 %fusion.167 = (bf16[1280,1120]{1,0:T(8,128)(2,1)S(1)}, f32[1280,1120]{1,0:T(8,128)}) fusion(bf16[1280,1120]{0,1:T(8,128)(2,1)S(1)} %get-tuple-element.156, bf16[1120,1120]{1,0:T(8,128)(2,1)S(1)} %bitcast.287), kind=kOutput, calls=%fused_computation.366 | convolution fusion | flops 3212697600 | bytes 13977600 | tf_op jit(solution)/shard_map/dot_general | solution.py:30
  299.2 27.1 %collective-permute-done.59 = bf16[1120,560]{0,1:T(8,128)(2,1)} collective-permute-done((bf16[1120,560]{0,1:T(8,128)(2,1)}, bf16[1120,560]{0,1:T(8,128)(2,1)}, u32[]{:S(2)}, u32[]{:S(2)}) %collective-permute-start.59) | collective-permute-done | bytes 1254432 | tf_op jit(solution)/shard_map/ppermute | solution.py:18
  326.3 5.5 fusion.12
  340.4 5.7 add_convert_fusion
  361.0 40.9 %collective-permute-done.61 = bf16[280,560]{1,0:T(8,128)(2,1)S(1)} collective-permute-done((bf16[280,560]{1,0:T(8,128)(2,1)S(1)}, bf16[280,560]{1,0:T(8,128)(2,1)S(1)}, u32[]{:S(2)}, u32[]{:S(2)}) %collective-permute-start.61) | collective-permute-done | bytes 313632 | tf_op jit(solution)/shard_map/ppermute | solution.py:61
  413.1 16.2 %collective-permute-done.64 = bf16[280,560]{1,0:T(8,128)(2,1)} collective-permute-done((bf16[280,560]{1,0:T(8,128)(2,1)S(1)}, bf16[280,560]{1,0:T(8,128)(2,1)}, u32[]{:S(2)}, u32[]{:S(2)}) %collective-permute-start.64) | collective-permute-done | bytes 313632 | tf_op jit(solution)/shard_map/ppermute | solution.py:18
  430.8 6.3 collective-permute-done.71
  440.6 11.3 %collective-permute-done.34 = bf16[320,1120]{1,0:T(8,128)(2,1)} collective-permute-done((bf16[320,1120]{1,0:T(8,128)(2,1)}, bf16[320,1120]{1,0:T(8,128)(2,1)}, u32[]{:S(2)}, u32[]{:S(2)}) %collective-permute-start.34) | collective-permute-done | bytes 716832 | tf_op jit(solution)/shard_map/ppermute | solution.py:18
  477.6 4.5 copy.198
  493.9 6.4 fusion.65
  500.4 5.7 multiply_reduce_fusion
  506.0 11.0 %multiply_convert_fusion = bf16[4,5,320,320]{2,3,1,0:T(8,128)(2,1)} fusion(f32[4,5,320,320]{2,3,1,0:T(8,128)} %get-tuple-element.152, f32[4,5,320]{2,1,0:T(8,128)} %get-tuple-element.151, f32[4,5,320,320]{2,3,1,0:T(8,128)} %get-tuple-element.142, f32[4,5,320]{2,1,0:T(8,128)} %copy-done.59), kind=kLoop, calls=%fused_computation.1 | loop fusion | flops 8192000 | bytes 20531200 | tf_op jit(solution)/shard_map/convert_element_type | solution.py:224
  517.0 5.1 fusion.72
  547.4 5.9 fusion.169
  559.2 11.5 %collective-permute-done.45 = bf16[4,144,840]{2,1,0:T(8,128)(2,1)} collective-permute-done((bf16[4,144,840]{2,1,0:T(8,128)(2,1)}, bf16[4,144,840]{2,1,0:T(8,128)(2,1)}, u32[]{:S(2)}, u32[]{:S(2)}) %collective-permute-start.45) | collective-permute-done | bytes 967712 | tf_op jit(solution)/shard_map/ppermute | solution.py:18
  588.5 8.4 %collective-permute-done.47 = bf16[144,840]{1,0:T(8,128)(2,1)S(1)} collective-permute-done((bf16[144,840]{1,0:T(8,128)(2,1)S(1)}, bf16[144,840]{1,0:T(8,128)(2,1)S(1)}, u32[]{:S(2)}, u32[]{:S(2)}) %collective-permute-start.47) | collective-permute-done | bytes 241952 | tf_op jit(solution)/shard_map/ppermute | solution.py:61
  621.2 7.1 %collective-permute-done.57 = bf16[1,140,280]{2,0,1:T(2,128)(2,1)} collective-permute-done((bf16[1,140,280]{2,0,1:T(2,128)(2,1)}, bf16[1,140,280]{2,0,1:T(2,128)(2,1)}, u32[]{:S(2)}, u32[]{:S(2)}) %collective-permute-start.57) | collective-permute-done | bytes 78432 | tf_op jit(solution)/shard_map/ppermute | solution.py:61
  (501 shorter events, 305.0 us)
Async XLA Ops:
  0.6 51.3 %collective-permute-start.10 = (s32[1]{0:T(128)}, s32[1]{0:T(128)}, u32[]{:S(2)}, u32[]{:S(2)}) collective-permute-start(s32[1]{0:T(128)} %param.18), channel_id=1, source_target_pairs={{0,4},{4,0},{1,5},{5,1},{2,6},{6,2},{3,7},{7,3},{8,12},{12,8},{9,1... | collective-permute-start | bytes 20 | tf_op jit(solution)/shard_map/ppermute | solution.py:18
  1.2 53.6 %collective-permute-start.11 = (s32[1]{0:T(128)}, s32[1]{0:T(128)}, u32[]{:S(2)}, u32[]{:S(2)}) collective-permute-start(s32[1]{0:T(128)} %param.18), channel_id=1, source_target_pairs={{0,8},{8,0},{1,9},{9,1},{2,10},{10,2},{3,11},{11,3},{4,12},{12,4},... | collective-permute-start | bytes 20 | tf_op jit(solution)/shard_map/ppermute | solution.py:18
  10.7 49.5 %collective-permute-start.2 = (bf16[12,280]{1,0:T(8,128)(2,1)}, bf16[12,280]{1,0:T(8,128)(2,1)}, u32[]{:S(2)}, u32[]{:S(2)}) collective-permute-start(bf16[12,280]{1,0:T(8,128)(2,1)} %reshape.415), channel_id=1, source_target_pairs={{0,3},{1,0},{2,1},{3,2},{4,7},{5,4},{6,5},{7,6},{8,11},{9,8},{10,9... | collective-permute-start | bytes 20168 | tf_op jit(solution)/shard_map/ppermute | solution.py:61
  14.3 45.9 %collective-permute-start.1 = (bf16[12,280]{1,0:T(8,128)(2,1)}, bf16[12,280]{1,0:T(8,128)(2,1)}, u32[]{:S(2)}, u32[]{:S(2)}) collective-permute-start(bf16[12,280]{1,0:T(8,128)(2,1)} %reshape.415), channel_id=1, source_target_pairs={{0,2},{1,3},{2,0},{3,1},{4,6},{5,7},{6,4},{7,5},{8,10},{9,11},{10,... | collective-permute-start | bytes 20168 | tf_op jit(solution)/shard_map/ppermute | solution.py:61
  14.3 49.8 %collective-permute-start = (bf16[12,280]{1,0:T(8,128)(2,1)}, bf16[12,280]{1,0:T(8,128)(2,1)}, u32[]{:S(2)}, u32[]{:S(2)}) collective-permute-start(bf16[12,280]{1,0:T(8,128)(2,1)} %reshape.415), channel_id=1, source_target_pairs={{0,1},{1,2},{2,3},{3,0},{4,5},{5,6},{6,7},{7,4},{8,9},{9,10},{10,1... | collective-permute-start | bytes 20168 | tf_op jit(solution)/shard_map/ppermute | solution.py:61
  66.5 60.4 %collective-permute-start.26 = (bf16[280,1120]{1,0:T(8,128)(2,1)}, bf16[280,1120]{1,0:T(8,128)(2,1)S(1)}, u32[]{:S(2)}, u32[]{:S(2)}) collective-permute-start(bf16[280,1120]{1,0:T(8,128)(2,1)} %get-tuple-element.54), channel_id=1, source_target_pairs={{0,3},{1,0},{2,1},{3,2},{4,7},{5,4},{6,5},{7,6},{8,11},{9,8},{10,9... | collective-permute-start | bytes 1881608 | tf_op jit(solution)/shard_map/ppermute | solution.py:61
  67.5 76.5 %collective-permute-start.25 = (bf16[280,1120]{1,0:T(8,128)(2,1)}, bf16[280,1120]{1,0:T(8,128)(2,1)S(1)}, u32[]{:S(2)}, u32[]{:S(2)}) collective-permute-start(bf16[280,1120]{1,0:T(8,128)(2,1)} %get-tuple-element.54), channel_id=1, source_target_pairs={{0,2},{1,3},{2,0},{3,1},{4,6},{5,7},{6,4},{7,5},{8,10},{9,11},{10,... | collective-permute-start | bytes 1881608 | tf_op jit(solution)/shard_map/ppermute | solution.py:61
  71.2 73.3 %collective-permute-start.24 = (bf16[280,1120]{1,0:T(8,128)(2,1)}, bf16[280,1120]{1,0:T(8,128)(2,1)S(1)}, u32[]{:S(2)}, u32[]{:S(2)}) collective-permute-start(bf16[280,1120]{1,0:T(8,128)(2,1)} %get-tuple-element.54), channel_id=1, source_target_pairs={{0,1},{1,2},{2,3},{3,0},{4,5},{5,6},{6,7},{7,4},{8,9},{9,10},{10,1... | collective-permute-start | bytes 1881608 | tf_op jit(solution)/shard_map/ppermute | solution.py:61
  74.2 50.8 %collective-permute-start.6 = (bf16[144,840]{1,0:T(8,128)(2,1)}, bf16[144,840]{1,0:T(8,128)(2,1)}, u32[]{:S(2)}, u32[]{:S(2)}) collective-permute-start(bf16[144,840]{1,0:T(8,128)(2,1)} %select_n.382), channel_id=1, source_target_pairs={{0,1},{1,2},{2,3},{3,0},{4,5},{5,6},{6,7},{7,4},{8,9},{9,10},{10,1... | collective-permute-start | bytes 725768 | tf_op jit(solution)/shard_map/ppermute | solution.py:61
  83.5 62.7 %collective-permute-start.19 = (bf16[3,2,40,1120]{3,2,0,1:T(8,128)(2,1)}, bf16[3,2,40,1120]{3,2,0,1:T(8,128)(2,1)}, u32[]{:S(2)}, u32[]{:S(2)}) collective-permute-start(bf16[3,2,40,1120]{3,2,0,1:T(8,128)(2,1)} %pad_maximum_fusion.20), channel_id=1, source_target_pairs={{0,8},{8,0},{1,9},{9,1},{2,10},{10,2},{3,11},{11,3},{4,12},{12,4},... | collective-permute-start | bytes 1612808 | tf_op jit(solution)/shard_map/ppermute | solution.py:18
  126.8 74.6 %collective-permute-start.30 = (bf16[320,1120]{1,0:T(8,128)(2,1)}, bf16[320,1120]{1,0:T(8,128)(2,1)}, u32[]{:S(2)}, u32[]{:S(2)}) collective-permute-start(bf16[320,1120]{1,0:T(8,128)(2,1)} %fusion.44), channel_id=1, source_target_pairs={{0,4},{4,0},{1,5},{5,1},{2,6},{6,2},{3,7},{7,3},{8,12},{12,8},{9,1... | collective-permute-start | bytes 2150408 | tf_op jit(solution)/shard_map/ppermute | solution.py:18
  150.1 90.3 %collective-permute-start.27 = (bf16[3,280,1120]{2,1,0:T(8,128)(2,1)}, bf16[3,280,1120]{2,1,0:T(8,128)(2,1)}, u32[]{:S(2)}, u32[]{:S(2)}) collective-permute-start(bf16[3,280,1120]{2,1,0:T(8,128)(2,1)} %pad_maximum_fusion.7), channel_id=1, source_target_pairs={{0,16},{16,0},{1,17},{17,1},{2,18},{18,2},{3,19},{19,3},{4,20},{20... | collective-permute-start | bytes 5644808 | tf_op jit(solution)/shard_map/ppermute | solution.py:18
  162.5 39.0 %collective-permute-start.32 = (bf16[320,1120]{1,0:T(8,128)(2,1)}, bf16[320,1120]{1,0:T(8,128)(2,1)}, u32[]{:S(2)}, u32[]{:S(2)}) collective-permute-start(bf16[320,1120]{1,0:T(8,128)(2,1)} %collective-permute-done.31), channel_id=1, source_target_pairs={{0,4},{4,0},{1,5},{5,1},{2,6},{6,2},{3,7},{7,3},{8,12},{12,8},{9,1... | collective-permute-start | bytes 2150408 | tf_op jit(solution)/shard_map/ppermute | solution.py:18
  168.6 62.6 %collective-permute-start.20 = (bf16[3,4,40,1120]{3,2,0,1:T(8,128)(2,1)}, bf16[3,4,40,1120]{3,2,0,1:T(8,128)(2,1)}, u32[]{:S(2)}, u32[]{:S(2)}) collective-permute-start(bf16[3,4,40,1120]{3,2,0,1:T(8,128)(2,1)} %pad_maximum_fusion.13), channel_id=1, source_target_pairs={{0,16},{16,0},{1,17},{17,1},{2,18},{18,2},{3,19},{19,3},{4,20},{20... | collective-permute-start | bytes 3225608 | tf_op jit(solution)/shard_map/ppermute | solution.py:18
  268.0 72.5 %collective-permute-start.66 = (bf16[1120,560]{0,1:T(8,128)(2,1)}, bf16[1120,560]{0,1:T(8,128)(2,1)}, u32[]{:S(2)}, u32[]{:S(2)}) collective-permute-start(bf16[1120,560]{0,1:T(8,128)(2,1)} %convolution_convert_fusion.2), channel_id=1, source_target_pairs={{0,16},{16,0},{1,17},{17,1},{2,18},{18,2},{3,19},{19,3},{4,20},{20... | collective-permute-start | bytes 3763208 | tf_op jit(solution)/shard_map/ppermute | solution.py:18
  288.3 38.0 %collective-permute-start.59 = (bf16[1120,560]{0,1:T(8,128)(2,1)}, bf16[1120,560]{0,1:T(8,128)(2,1)}, u32[]{:S(2)}, u32[]{:S(2)}) collective-permute-start(bf16[1120,560]{0,1:T(8,128)(2,1)} %convolution_convert_fusion.1), channel_id=1, source_target_pairs={{0,16},{16,0},{1,17},{17,1},{2,18},{18,2},{3,19},{19,3},{4,20},{20... | collective-permute-start | bytes 3763208 | tf_op jit(solution)/shard_map/ppermute | solution.py:18
  290.2 59.9 %collective-permute-start.28 = (bf16[2,320,1120]{2,1,0:T(8,128)(2,1)}, bf16[2,320,1120]{2,1,0:T(8,128)(2,1)}, u32[]{:S(2)}, u32[]{:S(2)}) collective-permute-start(bf16[2,320,1120]{2,1,0:T(8,128)(2,1)} %pad_maximum_fusion.8), channel_id=1, source_target_pairs={{0,4},{4,0},{1,5},{5,1},{2,6},{6,2},{3,7},{7,3},{8,12},{12,8},{9,1... | collective-permute-start | bytes 4300808 | tf_op jit(solution)/shard_map/ppermute | solution.py:18
  298.6 110.1 %collective-permute-start.33 = (bf16[2,320,1120]{2,1,0:T(8,128)(2,1)}, bf16[2,320,1120]{2,1,0:T(8,128)(2,1)}, u32[]{:S(2)}, u32[]{:S(2)}) collective-permute-start(bf16[2,320,1120]{2,1,0:T(8,128)(2,1)} %pad_maximum_fusion.9), channel_id=1, source_target_pairs={{0,4},{4,0},{1,5},{5,1},{2,6},{6,2},{3,7},{7,3},{8,12},{12,8},{9,1... | collective-permute-start | bytes 4300808 | tf_op jit(solution)/shard_map/ppermute | solution.py:18
  350.1 54.6 %collective-permute-start.67 = (bf16[280,560]{1,0:T(8,128)(2,1)S(1)}, bf16[280,560]{1,0:T(8,128)(2,1)S(1)}, u32[]{:S(2)}, u32[]{:S(2)}) collective-permute-start(bf16[280,560]{1,0:T(8,128)(2,1)S(1)} %get-tuple-element.76), channel_id=1, source_target_pairs={{0,1},{1,2},{2,3},{3,0},{4,5},{5,6},{6,7},{7,4},{8,9},{9,10},{10,1... | collective-permute-start | bytes 940808 | tf_op jit(solution)/shard_map/ppermute | solution.py:61
  350.2 55.2 %collective-permute-start.69 = (bf16[280,560]{1,0:T(8,128)(2,1)S(1)}, bf16[280,560]{1,0:T(8,128)(2,1)S(1)}, u32[]{:S(2)}, u32[]{:S(2)}) collective-permute-start(bf16[280,560]{1,0:T(8,128)(2,1)S(1)} %get-tuple-element.77), channel_id=1, source_target_pairs={{0,3},{1,0},{2,1},{3,2},{4,7},{5,4},{6,5},{7,6},{8,11},{9,8},{10,9... | collective-permute-start | bytes 940808 | tf_op jit(solution)/shard_map/ppermute | solution.py:61
  354.1 51.3 %collective-permute-start.68 = (bf16[280,560]{1,0:T(8,128)(2,1)S(1)}, bf16[280,560]{1,0:T(8,128)(2,1)S(1)}, u32[]{:S(2)}, u32[]{:S(2)}) collective-permute-start(bf16[280,560]{1,0:T(8,128)(2,1)S(1)} %get-tuple-element.78), channel_id=1, source_target_pairs={{0,2},{1,3},{2,0},{3,1},{4,6},{5,7},{6,4},{7,5},{8,10},{9,11},{10,... | collective-permute-start | bytes 940808 | tf_op jit(solution)/shard_map/ppermute | solution.py:61
  358.3 43.7 %collective-permute-start.61 = (bf16[280,560]{1,0:T(8,128)(2,1)S(1)}, bf16[280,560]{1,0:T(8,128)(2,1)S(1)}, u32[]{:S(2)}, u32[]{:S(2)}) collective-permute-start(bf16[280,560]{1,0:T(8,128)(2,1)S(1)} %copy-done.46), channel_id=1, source_target_pairs={{0,2},{1,3},{2,0},{3,1},{4,6},{5,7},{6,4},{7,5},{8,10},{9,11},{10,... | collective-permute-start | bytes 940808 | tf_op jit(solution)/shard_map/ppermute | solution.py:61
  402.0 52.5 %collective-permute-start.29 = (bf16[320,1120]{1,0:T(8,128)(2,1)}, bf16[320,1120]{1,0:T(8,128)(2,1)}, u32[]{:S(2)}, u32[]{:S(2)}) collective-permute-start(bf16[320,1120]{1,0:T(8,128)(2,1)} %fusion.37), channel_id=1, source_target_pairs={{0,8},{8,0},{1,9},{9,1},{2,10},{10,2},{3,11},{11,3},{4,12},{12,4},... | collective-permute-start | bytes 2150408 | tf_op jit(solution)/shard_map/ppermute | solution.py:18
  405.4 31.6 %collective-permute-start.63 = (bf16[280,560]{1,0:T(8,128)(2,1)S(1)}, bf16[280,560]{1,0:T(8,128)(2,1)}, u32[]{:S(2)}, u32[]{:S(2)}) collective-permute-start(bf16[280,560]{1,0:T(8,128)(2,1)S(1)} %fusion.83), channel_id=1, source_target_pairs={{0,4},{4,0},{1,5},{5,1},{2,6},{6,2},{3,7},{7,3},{8,12},{12,8},{9,1... | collective-permute-start | bytes 940808 | tf_op jit(solution)/shard_map/ppermute | solution.py:18
  407.3 29.7 %collective-permute-start.71 = (bf16[280,560]{1,0:T(8,128)(2,1)}, bf16[280,560]{1,0:T(8,128)(2,1)}, u32[]{:S(2)}, u32[]{:S(2)}) collective-permute-start(bf16[280,560]{1,0:T(8,128)(2,1)} %fusion.80), channel_id=1, source_target_pairs={{0,8},{8,0},{1,9},{9,1},{2,10},{10,2},{3,11},{11,3},{4,12},{12,4},... | collective-permute-start | bytes 940808 | tf_op jit(solution)/shard_map/ppermute | solution.py:18
  411.3 40.6 %collective-permute-start.34 = (bf16[320,1120]{1,0:T(8,128)(2,1)}, bf16[320,1120]{1,0:T(8,128)(2,1)}, u32[]{:S(2)}, u32[]{:S(2)}) collective-permute-start(bf16[320,1120]{1,0:T(8,128)(2,1)} %fusion.35), channel_id=1, source_target_pairs={{0,8},{8,0},{1,9},{9,1},{2,10},{10,2},{3,11},{11,3},{4,12},{12,4},... | collective-permute-start | bytes 2150408 | tf_op jit(solution)/shard_map/ppermute | solution.py:18
  429.3 45.1 %collective-permute-start.70 = (bf16[280,560]{1,0:T(8,128)(2,1)}, bf16[280,560]{1,0:T(8,128)(2,1)}, u32[]{:S(2)}, u32[]{:S(2)}) collective-permute-start(bf16[280,560]{1,0:T(8,128)(2,1)} %fusion.80), channel_id=1, source_target_pairs={{0,4},{4,0},{1,5},{5,1},{2,6},{6,2},{3,7},{7,3},{8,12},{12,8},{9,1... | collective-permute-start | bytes 940808 | tf_op jit(solution)/shard_map/ppermute | solution.py:18
  437.0 48.5 %collective-permute-start.65 = (bf16[280,560]{1,0:T(8,128)(2,1)}, bf16[280,560]{1,0:T(8,128)(2,1)}, u32[]{:S(2)}, u32[]{:S(2)}) collective-permute-start(bf16[280,560]{1,0:T(8,128)(2,1)} %collective-permute-done.64), channel_id=1, source_target_pairs={{0,4},{4,0},{1,5},{5,1},{2,6},{6,2},{3,7},{7,3},{8,12},{12,8},{9,1... | collective-permute-start | bytes 940808 | tf_op jit(solution)/shard_map/ppermute | solution.py:18
  437.0 37.4 %collective-permute-start.72 = (bf16[280,560]{1,0:T(8,128)(2,1)}, bf16[280,560]{1,0:T(8,128)(2,1)}, u32[]{:S(2)}, u32[]{:S(2)}) collective-permute-start(bf16[280,560]{1,0:T(8,128)(2,1)} %collective-permute-done.71), channel_id=1, source_target_pairs={{0,4},{4,0},{1,5},{5,1},{2,6},{6,2},{3,7},{7,3},{8,12},{12,8},{9,1... | collective-permute-start | bytes 940808 | tf_op jit(solution)/shard_map/ppermute | solution.py:18
  474.4 79.1 %collective-permute-start.53 = (bf16[1,2,2,140,1120]{4,2,3,1,0:T(2,128)(2,1)}, bf16[1,2,2,140,1120]{4,2,3,1,0:T(2,128)(2,1)}, u32[]{:S(2)}, u32[]{:S(2)}) collective-permute-start(bf16[1,2,2,140,1120]{4,2,3,1,0:T(2,128)(2,1)} %copy.187), channel_id=1, source_target_pairs={{0,4},{4,0},{1,5},{5,1},{2,6},{6,2},{3,7},{7,3},{8,12},{12,8},{9,1... | collective-permute-start | bytes 3763208 | tf_op jit(solution)/shard_map/ppermute | solution.py:18
  557.2 41.7 %collective-permute-start.37 = (bf16[2,320,1120]{2,1,0:T(8,128)(2,1)S(1)}, bf16[2,320,1120]{2,1,0:T(8,128)(2,1)S(1)}, u32[]{:S(2)}, u32[]{:S(2)}) collective-permute-start(bf16[2,320,1120]{2,1,0:T(8,128)(2,1)S(1)} %pad_maximum_fusion.10), channel_id=1, source_target_pairs={{0,4},{4,0},{1,5},{5,1},{2,6},{6,2},{3,7},{7,3},{8,12},{12,8},{9,1... | collective-permute-start | bytes 4300808 | tf_op jit(solution)/shard_map/ppermute | solution.py:18
  601.9 29.0 %collective-permute-start.38 = (bf16[320,1120]{1,0:T(8,128)(2,1)}, bf16[320,1120]{1,0:T(8,128)(2,1)}, u32[]{:S(2)}, u32[]{:S(2)}) collective-permute-start(bf16[320,1120]{1,0:T(8,128)(2,1)} %fusion.33), channel_id=1, source_target_pairs={{0,8},{8,0},{1,9},{9,1},{2,10},{10,2},{3,11},{11,3},{4,12},{12,4},... | collective-permute-start | bytes 2150408 | tf_op jit(solution)/shard_map/ppermute | solution.py:18
  (125 other events, 1266.6 us)

commit v2 on v1

v2 whole, which is shorter than its diff:
```python
import functools

import jax
import jax.numpy as jnp
from jax import lax
from jax.experimental import pallas as pl
from jax.experimental.pallas import tpu as pltpu
from jax.sharding import Mesh, PartitionSpec as P

HEADS = 20
EPSILON = 1e-05
FILL = -1000000000.0
BF = jnp.bfloat16
F32 = jnp.float32
AXES = ("o", "y", "x", "c", "z")
WIDE = ("o", "y", "x", "c")
SWAP = [(0, 1), (1, 0)]
GROUP = 4
MIB = 1024 * 1024


def swap(value, axis):
    return lax.ppermute(value, axis, SWAP)


def dot(first, second):
    return jnp.dot(first, second, preferred_element_type=F32)


def dot_left(first, second):
    return lax.dot_general(first, second, (((0,), (0,)), ((), ())), preferred_element_type=F32)


def dot_right(first, second):
    return lax.dot_general(first, second, (((1,), (1,)), ((), ())), preferred_element_type=F32)


def shape_of(dims, dtype):
    return jax.ShapeDtypeStruct(dims, dtype)


class Order:
    def __init__(self):
        self.token = None

    def __call__(self, body, outs, scalars, arrays, after=(), scratch=(), flops=0, mib=28, name=None):
        after = list(after) + ([] if self.token is None else [self.token])
        n_scalar, n_array, n_out = len(scalars), len(arrays), len(outs)

        def run(*refs):
            token = refs[n_scalar + n_array + len(after) + n_out]
            values = tuple(ref[0] for ref in refs[:n_scalar])
            rest = refs[n_scalar + n_array + len(after) :]
            token[...] = jnp.zeros(token.shape, F32)
            body(values, *refs[n_scalar : n_scalar + n_array], *rest[:n_out], *rest[n_out + 1 :])

        moved = sum(a.size * a.dtype.itemsize for a in arrays) + sum(a.size * a.dtype.itemsize for a in outs)
        *given, self.token = pl.pallas_call(
            run,
            out_shape=(*outs, shape_of((8, 128), F32)),
            in_specs=[pl.BlockSpec(memory_space=pltpu.SMEM)] * n_scalar
            + [pl.BlockSpec(memory_space=pltpu.VMEM)] * n_array
            + [pl.BlockSpec(memory_space=pl.ANY)] * len(after),
            out_specs=(pl.BlockSpec(memory_space=pltpu.VMEM),) * (n_out + 1),
            scratch_shapes=list(scratch),
            compiler_params=pltpu.CompilerParams(vmem_limit_bytes=mib * MIB),
            cost_estimate=pl.CostEstimate(flops=int(flops), bytes_accessed=int(moved), transcendentals=0),
            name=name,
        )(*scalars, *arrays, *after)
        return given


def group_gather(value):
    over_x = swap(value, "x")
    over_core = swap(value, "c")
    return [value, over_core, over_x, swap(over_x, "c")]


def depth_shift(value, shift, count):
    return lax.ppermute(value, "z", [(i, (i + shift) % count) for i in range(count)])


def depth_exchange(parts):
    return lax.all_to_all(parts, "z", 0, 0)


def depth_line(value, count):
    up, down = [], []
    for s in range(count - 1):
        up.append(lax.ppermute(up[-1] if s else value, "z", [(i, i + 1) for i in range(s, count - 1)]))
        down.append(lax.ppermute(down[-1] if s else value, "z", [(i, i - 1) for i in range(1, count - s)]))
    return up, down


def normal(values):
    center = values - jnp.mean(values, axis=-1, keepdims=True)
    spread = jnp.mean(center * center, axis=-1, keepdims=True)
    inverse = lax.rsqrt(spread + EPSILON)
    return center * inverse, inverse


def normal_back(grad, unit, inverse):
    return (
        grad
        - jnp.mean(grad, axis=-1, keepdims=True)
        - unit * jnp.mean(grad * unit, axis=-1, keepdims=True)
    ) * inverse


def when_each(index, count, step):
    for k in range(count):
        pl.when(index == k)(functools.partial(step, k))


def next_block(z, step, count):
    return z + 1 + step if step < count - 1 - z else count - 2 - step


def line_ref(z, other, up, down):
    return up[z - 1 - other] if other < z else down[other - z - 1]


def allowed_of(rows, length):
    query = lax.broadcasted_iota(jnp.int32, (rows, rows), 0)
    key = lax.broadcasted_iota(jnp.int32, (rows, rows), 1)
    return (key <= query) & (key < length)


def head_probs(query, key, allowed, scale):
    scores = jnp.where(allowed, dot_right(query, key) * scale, FILL)
    weights = jnp.exp(scores - jnp.max(scores, axis=1, keepdims=True))
    return weights * (1.0 / jnp.sum(weights, axis=1, keepdims=True))


def attend(heads, lengths, normed, full, query_shift, value_shift, joined, contexts):
    rows, part = normed[0].shape[0], full.shape[1] // 3
    head = part // heads
    scale = head ** (-0.5)
    for n, x in enumerate(normed):
        sums = dot(x[...], full[...])
        query = (sums[:, :part] + query_shift[...]).astype(BF)
        key = sums[:, part : 2 * part].astype(BF)
        value = (sums[:, 2 * part :] + value_shift[...]).astype(BF)
        joined[n, :, :part] = query
        joined[n, :, part : 2 * part] = key
        joined[n, :, 2 * part :] = value
        allowed = allowed_of(rows, lengths[n])
        out = []
        for h in range(heads):
            cut = slice(h * head, (h + 1) * head)
            probs = head_probs(query[:, cut], key[:, cut], allowed, scale).astype(BF)
            out.append(dot(probs, value[:, cut]))
        contexts[n][...] = jnp.concatenate(out, axis=1).astype(BF)


def attend_back(heads, lengths, joined, grad, out):
    rows, part = joined.shape[1], joined.shape[2] // 3
    head = part // heads
    scale = head ** (-0.5)
    for n in range(joined.shape[0]):
        query, key, value = (joined[n, :, p * part : (p + 1) * part] for p in range(3))
        above = grad[n][...]
        allowed = allowed_of(rows, lengths[n])
        found = ([], [], [])
        for h in range(heads):
            cut = slice(h * head, (h + 1) * head)
            q, k, v, g = query[:, cut], key[:, cut], value[:, cut], above[:, cut]
            probs = head_probs(q, k, allowed, scale)
            probs_grad = dot_right(g, v)
            found[2].append(dot_left(probs.astype(BF), g))
            score = probs * (probs_grad - jnp.sum(probs * probs_grad, axis=1, keepdims=True))
            score = score.astype(BF)
            found[0].append(dot(score, k) * scale)
            found[1].append(dot_left(score, q) * scale)
        out[n] = jnp.concatenate(found[0] + found[1] + found[2], axis=1).astype(BF)


def gelu_both(values):
    root = (2.0 / jnp.pi) ** 0.5
    square = values * values
    bend = jnp.tanh(root * (values + 0.044715 * (square * values)))
    half = 0.5 * (1.0 + bend)
    slope = half + 0.5 * values * (1.0 - bend * bend) * (root * (1.0 + 3.0 * 0.044715 * square))
    return values * half, slope


def column_sum(values):
    return jnp.sum(values, axis=0, keepdims=True)


def build(outer, depth):
    def shards(
        tokens, lengths, norm1_gain, norm1_bias, qkv_weight, query_bias, value_bias, out_weight,
        out_bias, norm2_gain, norm2_bias, up_weight, up_bias, down_weight, down_bias, cotangent,
    ):
        rows, width = tokens.shape
        heads = HEADS // GROUP
        part = width // GROUP
        part_depth = width // depth
        hidden_depth = up_weight.shape[1] // depth
        block = hidden_depth // GROUP
        mine = depth * block
        wide = outer * 2 * GROUP
        sides = outer * 2
        y, x, c, z = (lax.axis_index(name).astype(jnp.int32).reshape(1) for name in ("y", "x", "c", "z"))
        member = 2 * x + c
        others = range(1, depth)
        step = Order()

        row_low, row_full = shape_of((rows, width), BF), shape_of((rows, width), F32)
        row_pair = shape_of((2, rows, width), BF)
        row_sum = shape_of((1, width), F32)
        cell, pair = shape_of((rows, part), BF), shape_of((2, rows, part), BF)

        half = (part_depth // 2 + 15) // 16 * 16
        rest = part_depth - half
        half_shape = shape_of((half, 3 * part), BF)

        def take_qkv(s, weight, own, send):
            def columns(k):
                for p in range(3):
                    at = (p * GROUP + k) * part
                    own[:, p * part : (p + 1) * part] = weight[:, at : at + part]

            when_each(s[0], GROUP, columns)

            @pl.when(s[1] == 0)
            def _():
                send[...] = own[:half]

            @pl.when(s[1] == 1)
            def _():
                send[:rest] = own[half:]
                send[rest:] = jnp.zeros((half - rest, 3 * part), BF)

        qkv_own, qkv_half = step(
            take_qkv, [shape_of((part_depth, 3 * part), BF), half_shape], [member, y], [qkv_weight], name="take_qkv"
        )
        qkv_up, qkv_down = depth_line(qkv_half, depth)

        vectors = jnp.concatenate(
            [
                jnp.stack([norm1_gain, norm1_bias, query_bias, value_bias, out_bias, norm2_gain, norm2_bias, down_bias]),
                up_bias.reshape(GROUP, block),
            ]
        )
        vectors = [vectors] + [depth_shift(vectors, r, depth) for r in others]

        def norm_one(s, values, *refs):
            blocks, (normed, whole, up_shift, query_shift, value_shift) = refs[:depth], refs[depth:]

            def put(k):
                for r in range(depth):
                    at = (k - r) % depth * part_depth
                    whole[:, at : at + part_depth] = blocks[r][:8].astype(F32)

                    def of_member(m, r=r):
                        to = (k - r) % depth * block
                        up_shift[:, to : to + block] = blocks[r][8 + m : 9 + m].astype(F32)

                    when_each(s[1], GROUP, of_member)

            when_each(s[0], depth, put)

            def of_member(m):
                query_shift[...] = whole[2:3, m * part : (m + 1) * part]
                value_shift[...] = whole[3:4, m * part : (m + 1) * part]

            when_each(s[1], GROUP, of_member)
            normed[...] = (normal(values[...].astype(F32))[0] * whole[0:1] + whole[1:2]).astype(BF)

        normed_one, whole, up_shift, query_shift, value_shift = step(
            norm_one,
            [row_low, shape_of((8, width), F32), shape_of((1, mine), F32), shape_of((1, part), F32), shape_of((1, part), F32)],
            [z, member],
            [tokens, *vectors],
            name="norm_one",
        )
        normed_one_all = group_gather(normed_one)
        lengths_all = group_gather(lengths)

        def hand_on(up, down, like):
            came = []
            for s_at in others:

                def choose_block(s, *refs, at=s_at - 1):
                    ups, downs, out = refs[: at + 1], refs[at + 1 : -1], refs[-1]

                    def copy(k):
                        out[...] = line_ref(k, next_block(k, at, depth), ups, downs)[...]

                    when_each(s[0], depth, copy)

                (block_now,) = step(choose_block, [like], [z], [*up[:s_at], *down[:s_at]], name="hand_on")
                came.append(swap(block_now, "y"))
                yield came

        qkv_far = list(hand_on(qkv_up, qkv_down, half_shape))[-1]

        pieces = 2 * GROUP
        height = (part_depth // pieces + 7) // 8 * 8
        starts = [(p * (part_depth - height) // (pieces - 1)) // 8 * 8 for p in range(pieces - 1)] + [part_depth - height]
        ends = starts[1:] + [part_depth]

        turn_shape = shape_of((part_depth, mine), BF)

        def take_mlp(s, up, down, out, up_own, turn, piece):
            def part_of(k):
                for n in range(depth):
                    at = n * hidden_depth + k * block
                    up_own[:, n * block : (n + 1) * block] = up[:, at : at + block]

                @pl.when(s[1] == 1)
                def _():
                    turn[...] = down[k * block : (k + 1) * block]

                def piece_of(p):
                    piece[...] = out[starts[p] : starts[p] + height]

                when_each(s[0] + GROUP * s[1], pieces, piece_of)

            when_each(s[0], GROUP, part_of)

            @pl.when(s[1] == 0)
            def _():
                turn[...] = up_own[...]

        up_own, turn, out_piece = step(
            take_mlp,
            [turn_shape, turn_shape, shape_of((height, width), BF)],
            [member, y],
            [up_weight, down_weight, out_weight],
            name="take_mlp",
        )
        out_pieces = [depth_shift(out_piece, r, depth) for r in others]
        mlp_up, mlp_down = depth_line(turn, depth)
        mlp_far_steps = hand_on(mlp_up, mlp_down, turn_shape)

        def live(s, values, grads, low, sums):
            keep = (lax.broadcasted_iota(jnp.int32, (rows, 1), 0) < s[0]).astype(F32)
            kept = values[...].astype(F32) * keep
            grads[...] = kept
            low[...] = kept.astype(BF)
            sums[...] = column_sum(kept)

        grad_rows, grad_low, down_sum = step(
            live, [row_full, row_low, row_sum], [lengths], [cotangent], after=[normed_one_all[2]], name="live"
        )
        grad_all = group_gather(grad_low)

        attend_flops = 2 * rows * width * 3 * part * 2 + 2 * heads * 4 * rows * rows * 128
        lines = depth - 1

        def attend_far(s, own, *refs):
            ups, downs, handed = refs[:lines], refs[lines : 2 * lines], refs[2 * lines : 3 * lines]
            first, second, shift_q, shift_v, full, joined, context = refs[3 * lines :]

            def put(k):
                full[k * part_depth : (k + 1) * part_depth] = own[...]
                for at in range(lines):
                    other = next_block(k, at, depth)
                    low = other * part_depth

                    def both(side, low=low, at=at, other=other):
                        ours = line_ref(k, other, ups, downs)
                        top, bottom = (ours, handed[at]) if side == 0 else (handed[at], ours)
                        full[low : low + half] = top[...]
                        full[low + half : low + part_depth] = bottom[:rest]

                    when_each(s[1], 2, both)

            when_each(s[0], depth, put)
            attend(heads, s[2:], (first, second), full, shift_q, shift_v, joined, (context.at[0], context.at[1]))

        joined_shape = shape_of((2, rows, 3 * part), BF)
        qkv_full, joined_far, context_far = step(
            attend_far,
            [shape_of((width, 3 * part), BF), joined_shape, pair],
            [z, y, lengths_all[2], lengths_all[3]],
            [qkv_own, *qkv_up, *qkv_down, *qkv_far, normed_one_all[2], normed_one_all[3], query_shift, value_shift],
            flops=attend_flops,
            name="attend_far",
        )
        came_far = swap(context_far, "x")
        next(mlp_far_steps)

        def attend_near(s, full, first, second, shift_q, shift_v, joined, ours, theirs):
            attend(heads, s, (first, second), full, shift_q, shift_v, joined, (ours, theirs))

        joined_near, context_own, context_core = step(
            attend_near,
            [joined_shape, cell, cell],
            [lengths_all[0], lengths_all[1]],
            [qkv_full, normed_one_all[0], normed_one_all[1], query_shift, value_shift],
            flops=attend_flops,
            name="attend_near",
        )
        came_core = swap(context_core, "c")
        came_last = swap(came_far[1], "c")

        got = jnp.stack(out_pieces)
        spread = [got]
        for axis in ("c", "x", "y"):
            spread = spread + [swap(v, axis) for v in spread]

        def out_whole(s, own, *refs):
            blocks, full = refs[:-1], refs[-1]

            def put(k):
                full[k * part_depth : (k + 1) * part_depth] = own[...]

                def of_place(p):
                    for other in range(pieces):
                        q = p ^ other
                        for r in others:
                            at = (k - r) % depth * part_depth + starts[q]
                            full[at : at + ends[q] - starts[q]] = blocks[other][r - 1, : ends[q] - starts[q]]

                when_each(s[1] + GROUP * s[2], pieces, of_place)

            when_each(s[0], depth, put)

        (out_full,) = step(
            out_whole, [shape_of((width, width), BF)], [z, member, y], [out_weight, *spread], name="out_whole"
        )
        next(mlp_far_steps)

        def project(s, own, core, far_pair, last, full, values, vector, context, middle, normed):
            def put(k):
                for other, ref in enumerate((own, core, None, last)):
                    at = (k ^ other) * part
                    context[:, at : at + part] = far_pair[0] if ref is None else ref[...]

            when_each(s[0], GROUP, put)
            total = values[...].astype(F32) + (dot(context[...], full[...]) + vector[4:5])
            middle[...] = total
            normed[...] = (normal(total)[0] * vector[5:6] + vector[6:7]).astype(BF)

        context, middle, normed_two = step(
            project,
            [row_low, row_full, row_low],
            [member],
            [context_own, came_core, came_far, came_last, out_full, tokens, whole],
            flops=2 * rows * width * width,
            name="project",
        )
        normed_two_all = group_gather(normed_two)
        mlp_far = list(mlp_far_steps)[-1]

        def feed(s, up_ref, down_ref, *refs):
            ups, downs, handed = refs[:lines], refs[lines : 2 * lines], refs[2 * lines : 3 * lines]
            refs = refs[3 * lines :]
            normed, grads, shift = refs[:4], refs[4:8], refs[8]
            active, before, sums, down_full, two_own, two_core, two_far, up_full = refs[9:]

            def put(k):
                up_full[k * part_depth : (k + 1) * part_depth] = up_ref[...]

                def of_member(m):
                    down_full[k * block : (k + 1) * block] = down_ref[m * block : (m + 1) * block]

                when_each(s[2], GROUP, of_member)
                for at in range(lines):
                    other = next_block(k, at, depth)

                    def both(side, at=at, other=other):
                        ours = line_ref(k, other, ups, downs)
                        up_from, down_from = (ours, handed[at]) if side == 0 else (handed[at], ours)
                        up_full[other * part_depth : (other + 1) * part_depth] = up_from[...]
                        down_full[other * block : (other + 1) * block] = down_from[...]

                    when_each(s[1], 2, both)

            when_each(s[0], depth, put)
            total = jnp.zeros((1, mine), F32)
            for k in (3, 2, 1, 0):
                at = slice(k * rows, (k + 1) * rows)
                value, slope = gelu_both(dot(normed[k][...], up_full[...]) + shift[...])
                active[at] = value.astype(BF)
                grad = (dot_right(grads[k][...], down_full[...]) * slope).astype(BF)
                before[at] = grad
                total = total + column_sum(grad.astype(F32))
                two = dot_right(grad, up_full[...])
                if k == 0:
                    two_own[...] = two
                elif k == 2:
                    two_far[...] = two
                else:
                    two_core[k // 2] = two.astype(BF)
            sums[...] = total

        hidden_rows = shape_of((GROUP * rows, mine), BF)
        active, before, up_sums, down_full, two_own, two_core, two_far = step(
            feed,
            [hidden_rows, hidden_rows, shape_of((1, mine), F32), shape_of((mine, width), BF), row_full, row_pair, row_full],
            [z, y, member],
            [up_own, down_weight, *mlp_up, *mlp_down, *mlp_far, *normed_two_all, *grad_all, up_shift],
            scratch=[pltpu.VMEM((width, mine), BF)],
            flops=3 * 2 * GROUP * rows * width * mine,
            mib=52,
            name="feed",
        )
        two_came = swap(two_core, "c")

        each, side = mine // sides, width // sides

        def columns_for(value, count, index):
            cut = [value[:, (2 * o + index) * count : (2 * o + index + 1) * count] for o in range(outer)]
            return cut[0] if outer == 1 else jnp.concatenate(cut, axis=1)

        def weight_grad(left, right, count, came, name):
            n_left, n_right = len(left), len(right)
            out = shape_of((depth, left[0].shape[1] // depth, outer * count), BF)

            def body(s, *refs):
                lefts, rights = refs[:n_left], refs[n_left : n_left + n_right]
                refs = refs[n_left + n_right :]
                came_ref, (out_ref, *packed) = (None, refs) if came is None else (refs[0], refs[1:])
                left_all = lefts[0] if n_left == 1 else packed[0]
                right_all = packed[-1]
                for k in range(n_left if n_left > 1 else 0):
                    left_all[k * rows : (k + 1) * rows] = lefts[k][...]

                def pack(index):
                    for k, ref in enumerate(rights):
                        tall = ref.shape[0]
                        right_all[k * tall : (k + 1) * tall] = columns_for(ref, count, index)

                when_each(s[0], 2, lambda k: pack(1 - k if came is None else k))
                total = dot_left(left_all[...], right_all[...])
                tall = total.shape[0] // depth
                for n in range(depth):
                    piece = total[n * tall : (n + 1) * tall]
                    if came is not None:
                        piece = piece + came_ref[n].astype(F32)
                    out_ref[n] = piece.astype(BF)

            scratch = [pltpu.VMEM((GROUP * rows, outer * count), BF)]
            if n_left > 1:
                scratch = [pltpu.VMEM((GROUP * rows, left[0].shape[1]), BF)] + scratch
            (result,) = step(
                body, [out], [y], [*left, *right, *([] if came is None else [came])],
                scratch=scratch, flops=2 * GROUP * rows * left[0].shape[1] * outer * count, mib=32, name=name,
            )
            return result

        down_came = swap(weight_grad([active], grad_all, side, None, "down_send"), "y")

        def add_far(s, far, came, out):
            out[...] = (far[...] + came[1].astype(F32)).astype(BF)

        (two_sent,) = step(add_far, [row_low], [], [two_far, two_came], name="add_two")
        two_last = swap(two_sent, "x")
        up_came = swap(weight_grad(normed_two_all, [before], each, None, "up_send"), "y")

        def feed_out(s, active_ref, full, own, core, far_out):
            for k in range(GROUP):
                value = dot(active_ref[k * rows : (k + 1) * rows], full[...])
                if k == 0:
                    own[...] = value
                elif k == 2:
                    far_out[...] = value
                else:
                    core[k // 2] = value.astype(BF)

        mlp_own, mlp_core, mlp_away = step(
            feed_out, [row_full, row_pair, row_full], [], [active, down_full],
            flops=2 * GROUP * rows * width * mine, name="feed_out",
        )
        mlp_came = swap(mlp_core, "c")

        def turn_back(
            s, own, came, last, values, grads, vector, full,
            middle_grad, low, ours, core, far_pair, gain_sum, shift_sum, out_sum,
        ):
            two = own[...] + came[0].astype(F32) + last[...].astype(F32)
            unit, inverse = normal(values[...])
            gain_sum[...] = column_sum(two * unit)
            shift_sum[...] = column_sum(two)
            total = grads[...] + normal_back(two * vector[5:6], unit, inverse)
            middle_grad[...] = total
            low[...] = total.astype(BF)
            out_sum[...] = column_sum(total.astype(BF).astype(F32))
            grad = dot_right(low[...], full[...]).astype(BF)

            def split(k):
                for other in range(GROUP):
                    at = (k ^ other) * part
                    piece = grad[:, at : at + part]
                    if other == 0:
                        ours[...] = piece
                    elif other == 1:
                        core[...] = piece
                    else:
                        far_pair[other - 2] = piece

            when_each(s[0], GROUP, split)

        middle_grad, middle_low, grad_own, grad_core, grad_far, gain_two_sum, shift_two_sum, out_sum = step(
            turn_back,
            [row_full, row_low, cell, cell, pair, row_sum, row_sum, row_sum],
            [member],
            [two_own, two_came, two_last, middle, grad_rows, whole, out_full],
            flops=2 * rows * width * width,
            name="turn_back",
        )
        back_far = swap(grad_far, "x")
        back_core = swap(grad_core, "c")
        back_last = swap(back_far[1], "c")

        strip = width // wide

        def out_grad(s, low, values, send, keep):
            total = dot_left(low[...], values[...])

            def split(k):
                for q in range(wide // 2):
                    for core in range(2):
                        target = keep if core == k else send
                        at = (2 * q + core) * strip
                        target[q] = total[at : at + strip].astype(BF)

            when_each(s[0], 2, split)

        out_shape = shape_of((wide // 2, strip, width), BF)
        out_send, out_keep = step(
            out_grad, [out_shape, out_shape], [c], [middle_low, context], flops=2 * rows * width * width, name="out_grad"
        )
        out_came = swap(out_send, "c")

        def out_fold(flag, keep, came, span):
            count = keep.shape[0] // 2

            def body(s, kept, arrived, send, keep_out):
                def split(k):
                    for q in range(count):
                        at = q // span * 2 * span + q % span
                        for bit in range(2):
                            target = keep_out if bit == k else send
                            source = at + bit * span
                            target[q] = (kept[source].astype(F32) + arrived[source].astype(F32)).astype(BF)

                when_each(s[0], 2, split)

            out = shape_of((count, strip, width), BF)
            return step(body, [out, out], [flag], [keep, came], name="out_fold")

        down_parts = depth_exchange(weight_grad([active], grad_all, side, down_came, "down_keep"))
        out_send, out_keep = out_fold(x, out_keep, out_came, 1)
        out_came = swap(out_send, "x")
        (mlp_sent,) = step(add_far, [row_low], [], [mlp_away, mlp_came], name="add_mlp")
        mlp_last = swap(mlp_sent, "x")

        def attend_back_near(s, joined, first, second, out):
            attend_back(heads, s, joined, (first, second), out)

        def attend_back_far(s, joined, first, second, out):
            attend_back(heads, s, joined, (first.at[0], second), out)

        back_flops = 2 * heads * 2 * rows * rows * 5 * 128 * 2
        (joined_grad_near,) = step(
            attend_back_near, [joined_shape], [lengths_all[0], lengths_all[1]], [joined_near, grad_own, back_core],
            flops=back_flops, name="attend_back_near",
        )
        up_parts = depth_exchange(weight_grad(normed_two_all, [before], each, up_came, "up_keep"))
        out_send, out_keep = out_fold(y, out_keep, out_came, 1)
        out_came = swap(out_send, "y")
        (joined_grad_far,) = step(
            attend_back_far, [joined_shape], [lengths_all[2], lengths_all[3]], [joined_far, back_far, back_last],
            flops=back_flops, name="attend_back_far",
        )

        def qkv_grad(s, first, second, third, fourth, near_ref, far_ref, send, keep, sums, left_all, right_all):
            for k, ref in enumerate((first, second, third, fourth)):
                left_all[k * rows : (k + 1) * rows] = ref[...]
                right_all[k * rows : (k + 1) * rows] = (near_ref, far_ref)[k // 2][k % 2]
            sums[...] = column_sum(right_all[...].astype(F32))
            total = dot_left(left_all[...], right_all[...])

            def split(k):
                first_half, second_half = (keep, send) if k == 0 else (send, keep)
                for n in range(depth):
                    at = n * part_depth
                    first_half[n] = total[at : at + half].astype(BF)
                    second_half[n, :rest] = total[at + half : at + part_depth].astype(BF)
                    second_half[n, rest:] = jnp.zeros((half - rest, 3 * part), BF)

            when_each(s[0], 2, split)

        halves = shape_of((depth, half, 3 * part), BF)
        qkv_send, qkv_keep, joined_sums = step(
            qkv_grad,
            [halves, halves, shape_of((1, 3 * part), F32)],
            [y],
            [*normed_one_all, joined_grad_near, joined_grad_far],
            scratch=[pltpu.VMEM((GROUP * rows, width), BF), pltpu.VMEM((GROUP * rows, 3 * part), BF)],
            flops=2 * GROUP * rows * width * 3 * part,
            mib=32,
            name="qkv_grad",
        )
        qkv_came = swap(qkv_send, "y")

        def one_back(s, near_ref, far_ref, full, own, core, far_out):
            own[...] = dot_right(near_ref[0], full[...])
            core[0] = dot_right(near_ref[1], full[...]).astype(BF)
            far_out[...] = dot_right(far_ref[0], full[...])
            core[1] = dot_right(far_ref[1], full[...]).astype(BF)

        one_own, one_core, one_far = step(
            one_back, [row_full, row_pair, row_full], [], [joined_grad_near, joined_grad_far, qkv_full],
            flops=2 * GROUP * rows * width * 3 * part, name="one_back",
        )
        one_came = swap(one_core, "c")

        def leave(s, own, came, last, values, vector, out):
            keep = (lax.broadcasted_iota(jnp.int32, (rows, 1), 0) < s[0]).astype(F32)
            fed = own[...] + came[0].astype(F32) + last[...].astype(F32) + vector[7:8]
            out[...] = (keep * (values[...] + fed)).astype(BF)

        (block_out,) = step(
            leave, [row_low], [lengths], [mlp_own, mlp_came, mlp_last, middle, whole], name="leave"
        )
        (one_sent,) = step(add_far, [row_low], [], [one_far, one_came], name="add_one")
        one_last = swap(one_sent, "x")

        tall = max(block, part_depth)
        low_type = BF if outer == 1 else F32

        def feed_pieces(s, down_ref, up_ref, out):
            for at, ref in enumerate((down_ref, up_ref)):
                total = ref[0].astype(F32)
                for n in others:
                    total = total + ref[n].astype(F32)
                out[at] = total.astype(low_type)

        (feed_piece,) = step(
            feed_pieces, [shape_of((2, tall, outer * each), low_type)], [], [down_parts, up_parts], name="feed_pieces"
        )
        if outer > 1:
            feed_piece = feed_piece.reshape(2, tall, outer, each)
            feed_piece = lax.psum_scatter(feed_piece, "o", scatter_dimension=2, tiled=False).astype(BF)
        feed_all = group_gather(feed_piece)

        def qkv_fold(s, keep, came, out):
            for n in range(depth):
                out[n] = (keep[n].astype(F32) + came[n].astype(F32)).astype(BF)

        (qkv_parts,) = step(qkv_fold, [halves], [], [qkv_keep, qkv_came], name="qkv_fold")
        qkv_parts = depth_exchange(qkv_parts)

        def out_split(s, keep, came, out):
            for q in range(outer):
                total = keep[q].astype(F32) + came[q].astype(F32)
                for n in range(depth):
                    out[n, q] = total[:, n * part_depth : (n + 1) * part_depth].astype(BF)

        (out_parts,) = step(
            out_split, [shape_of((depth, outer, strip, part_depth), BF)], [], [out_keep, out_came], name="out_split"
        )
        out_parts = depth_exchange(out_parts)

        def finish(s, own, came, last, values, vector, middle_ref, out, gain_sum, shift_sum):
            one = own[...] + came[0].astype(F32) + last[...].astype(F32)
            unit, inverse = normal(values[...].astype(F32))
            gain_sum[...] = column_sum(one * unit)
            shift_sum[...] = column_sum(one)
            out[...] = middle_ref[...] + normal_back(one * vector[0:1], unit, inverse)

        input_grad, gain_one_sum, shift_one_sum = step(
            finish, [row_full, row_sum, row_sum], [],
            [one_own, one_came, one_last, tokens, whole, middle_grad], name="finish",
        )

        def vector_pack(s, gain_one, shift_one, joined, out_ref, gain_two, shift_two, down_ref, up_ref, packed, line):
            packed[...] = jnp.zeros(packed.shape, F32)
            line[...] = jnp.zeros(line.shape, F32)
            for k, ref in ((0, gain_one), (1, shift_one), (4, out_ref), (5, gain_two), (6, shift_two), (7, down_ref)):
                line[k : k + 1] = ref[...]

            def of_member(m):
                line[2:3, m * part : (m + 1) * part] = joined[:, :part]
                line[3:4, m * part : (m + 1) * part] = joined[:, 2 * part :]
                for n in range(depth):
                    packed[n, 8 + m : 9 + m] = up_ref[:, n * block : (n + 1) * block]

            when_each(s[0], GROUP, of_member)
            for n in range(depth):
                packed[n, :8] = line[:, n * part_depth : (n + 1) * part_depth]

        (packed,) = step(
            vector_pack,
            [shape_of((depth, 8 + GROUP, part_depth), F32)],
            [member],
            [gain_one_sum, shift_one_sum, joined_sums, out_sum, gain_two_sum, shift_two_sum, down_sum, up_sums],
            scratch=[pltpu.VMEM((8, width), F32)],
            name="vector_pack",
        )
        packed = jnp.sum(depth_exchange(packed), axis=0)
        for axis in ("c", "x", "y"):
            packed = packed + swap(packed, axis)
        if outer > 1:
            packed = lax.psum(packed, "o")

        ratio = wide // depth
        fold = GROUP // ratio

        def feed_grads(s, *refs):
            blocks, (down_out, up_out) = refs[:4], refs[4:]

            def of_member(k):
                for m in range(GROUP):
                    cut = blocks[k ^ m][0, :, k * (side // GROUP) : (k + 1) * (side // GROUP)]
                    down_out[m * block : (m + 1) * block] = cut.astype(F32)
                for f in range(fold):
                    source = k % ratio * fold + f
                    at = k // ratio * block
                    up_out[:, f * block : (f + 1) * block] = blocks[k ^ source][1, :, at : at + block].astype(F32)

            when_each(s[0], GROUP, of_member)

        down_weight_grad, up_weight_grad = step(
            feed_grads,
            [shape_of((hidden_depth, side // GROUP), F32), shape_of((part_depth, fold * block), F32)],
            [member],
            feed_all,
            name="feed_grads",
        )

        def qkv_sum(s, parts, out):
            total = parts[0].astype(F32)
            for n in others:
                total = total + parts[n].astype(F32)
            out[...] = total.astype(BF)

        (qkv_piece,) = step(qkv_sum, [half_shape], [], [qkv_parts], name="qkv_sum")
        qkv_all = group_gather(qkv_piece)
        span = 3 * width // wide

        def qkv_columns(s, *refs):
            blocks, (keep, send) = refs[:4], refs[4:]

            def of_member(k):
                for o in range(outer):
                    for side_at in range(2):
                        cut, at = [], ((2 * o + side_at) * GROUP + k) * span
                        stop = at + span
                        while at < stop:
                            to = min(stop, (at // part + 1) * part)
                            p, m = divmod(at // part, GROUP)
                            low = p * part + at % part
                            cut.append(blocks[k ^ m][:, low : low + to - at])
                            at = to
                        found = cut[0] if len(cut) == 1 else jnp.concatenate(cut, axis=1)

                        def put(here, found=found, side_at=side_at, o=o):
                            target = keep if here == side_at else send
                            target[o] = found

                        when_each(s[1], 2, put)

            when_each(s[0], GROUP, of_member)

        span_shape = shape_of((outer, half, span), BF)
        qkv_keep, qkv_send = step(
            qkv_columns, [span_shape, span_shape], [member, y], qkv_all, name="qkv_columns"
        )
        if outer > 1:
            qkv_keep, qkv_send = (
                lax.psum_scatter(v.astype(F32), "o", scatter_dimension=0, tiled=True).astype(BF)
                for v in (qkv_keep, qkv_send)
            )
        qkv_came = swap(qkv_send, "y")

        def out_last(s, parts, out):
            total = parts[0].astype(F32)
            for n in others:
                total = total + parts[n].astype(F32)
            out[...] = total

        (out_sums,) = step(out_last, [shape_of((outer, strip, part_depth), F32)], [], [out_parts], name="out_last")
        out_sums = out_sums[0] if outer == 1 else lax.psum_scatter(out_sums, "o", scatter_dimension=0, tiled=False)
        out_weight_grad = out_sums.T

        def qkv_rows(s, keep, came, out):
            def put(k):
                top, bottom = (keep, came) if k == 0 else (came, keep)
                out[:half] = top[0].astype(F32)
                out[half:] = bottom[0, :rest].astype(F32)

            when_each(s[0], 2, put)

        (qkv_weight_grad,) = step(
            qkv_rows, [shape_of((part_depth, span), F32)], [y], [qkv_keep, qkv_came], name="qkv_rows"
        )
        return (
            block_out, input_grad, packed[0], packed[1], qkv_weight_grad, packed[2], packed[3], out_weight_grad,
            packed[4], packed[5], packed[6], up_weight_grad, packed[8:].reshape(hidden_depth), down_weight_grad, packed[7],
        )

    return shards


def solution(mesh):
    wide, depth = mesh.shape["wide"], mesh.shape["narrow"]
    outer = wide // 8
    fine = Mesh(mesh.devices.reshape(outer, 2, 2, 2, depth), AXES)
    rows, vec, mat = P(AXES, None), P("z"), P("z", None)
    placed = (
        rows, P(AXES), vec, vec, mat, vec, vec, mat, vec, vec, vec, mat, vec, mat, vec, rows,
    )
    grad = P("z", WIDE)
    return jax.shard_map(
        build(outer, depth),
        mesh=fine,
        in_specs=placed,
        out_specs=(rows, rows, vec, vec, grad, vec, vec, grad, vec, vec, vec, grad, vec, grad, vec),
        check_vma=False,
    )
```

time: 666 us -> 433 us (0.65)
  Pallas kernels: 0 us -> 109 us
  matrix products: 96.7 us -> 0 us
  other arithmetic: 91.7 us -> 0.07 us
  waiting for transfers between devices: 256 us -> 172 us
  local copies, waits for them, and re-layouts: 131 us -> 49.5 us
  blocking collectives: 0 us -> 10.4 us
    ppermute x27 -> x6, waiting for transfers between devices: 127 us -> 8.45 us  [depth_shift(): lax.ppermute(value, 'z', [(i, (i + shift) % count) for i in range(count)])]
    pallas_call x0 -> x42, Pallas kernels: none -> 109 us  [__call__(): pl.pallas_call(run, out_shape=(*outs, shape_of((8, 128), F32)), in_specs=...]
    dot_general x19 -> x0, matrix products: 87.9 us -> none  [the longest x6 23.9 us: dot_left(): lax.dot_general(first, second, (((0,), (0,)), ((), ())), preferred_elemen...]
    reshape x23 -> x2, local copies, waits for them, and re-layouts: 43.9 us -> 1.45 us  [the longest x1 0.77 us: shards(): up_bias.reshape(GROUP, block)]
    convert_element_type x21 -> x0, other arithmetic: 37.8 us -> none  [the longest x1 11 us: shards(): score_grad = score_grad.astype(BF)]
    ppermute x27 -> x6, starting transfers between devices: 44.3 us -> 8.8 us  [depth_shift(): lax.ppermute(value, 'z', [(i, (i + shift) % count) for i in range(count)])]
    unnamed x182 -> x209, local copies, waits for them, and re-layouts: 9.75 us -> 38.2 us
    ppermute x0 -> x12, waiting for transfers between devices: none -> 24.5 us  [the longest x6 24.3 us: depth_line(): lax.ppermute(down[-1] if s else value, 'z', [(i, i - 1) for i in range(1,...]
  transfers between devices with their start and end apart: 73 -> 75, of which waited for: 27 -> 29; matrix products, arithmetic and copies ran while one was open for 46% -> 1% of each run, Pallas kernels for 0% -> 20%
where the time goes in v2:
time: 433 us; the launch traced here: 425 us
  waiting for transfers between devices  172 us (40%)
  Pallas kernels  109 us (25%)
  starting transfers between devices  80.9 us (19%)
  local copies, waits for them, and re-layouts  49.5 us (11%)
  blocking collectives  10.4 us (2%)
    ppermute x53, waiting for transfers between devices, swap(): return lax.ppermute(value, axis, SWAP)  139 us
    pallas_call x42, Pallas kernels, __call__(): pl.pallas_call(run, out_shape=(*outs, shape_of((8, 128), F32)), in_specs=...  109 us
    unnamed x209, local copies, waits for them, and re-layouts  38.2 us
    ppermute x53, starting transfers between devices, swap(): return lax.ppermute(value, axis, SWAP)  37.8 us
    ppermute x6, waiting for transfers between devices, depth_line(): lax.ppermute(down[-1] if s else value, 'z', [(i, i - 1) for i in range(1,...  24.3 us
    all_to_all x4, starting transfers between devices, depth_exchange(): return lax.all_to_all(parts, 'z', 0, 0)  18 us
    all_to_all x1, blocking collectives, depth_exchange(): return lax.all_to_all(parts, 'z', 0, 0)  10.4 us
    ppermute x6, starting transfers between devices, depth_shift(): lax.ppermute(value, 'z', [(i, (i + shift) % count) for i in range(count)])  8.8 us
  transfers between devices with their start and end apart: 75, of which 29 were waited for; matrix products, arithmetic and copies ran while one was open for 1% of the time, Pallas kernels for 20%

profile of v2, /device:TPU:0, one launch (start us, length us, event | category | flops | bytes accessed | tf_op | source)
XLA Modules:
  0.0 424.9 jit_solution(9663250241831712385)
XLA Ops:
  7.0 5.1 %collective-permute-start.8 = (bf16[12,280]{1,0:T(8,128)(2,1)S(1)}, bf16[12,280]{1,0:T(8,128)(2,1)S(1)}, u32[]{:S(2)}, u32[]{:S(2)}) collective-permute-start(bf16[12,280]{1,0:T(8,128)(2,1)S(1)} %concatenate.3.refs_3_), channel_id=1, source_target_pairs={{0,3},{1,0},{2,1},{3,2},{4,7},{5,4},{6,5},{7,6},{8,11},{9,8},{10,9... | collective-permute-start | bytes 20168 | tf_op jit(solution)/shard_map/ppermute | solution.py:80
  21.6 4.6 %collective-permute-start = (bf16[144,840]{1,0:T(8,128)(2,1)S(1)}, bf16[144,840]{1,0:T(8,128)(2,1)S(1)}, u32[]{:S(2)}, u32[]{:S(2)}) collective-permute-start(bf16[144,840]{1,0:T(8,128)(2,1)S(1)} %get-tuple-element.139), channel_id=1, source_target_pairs={{0,1},{1,2},{2,3},{4,5},{5,6},{6,7},{8,9},{9,10},{10,11},{12,13},{... | collective-permute-start | bytes 725768 | tf_op jit(solution)/shard_map/ppermute | solution.py:90
  30.6 5.0 %collective-permute-done.20.refs_2_.refs_14_.refs_3_ = bf16[320,1120]{1,0:T(8,128)(2,1)S(1)} collective-permute-done((bf16[320,1120]{1,0:T(8,128)(2,1)S(1)}, bf16[320,1120]{1,0:T(8,128)(2,1)S(1)}, u32[]{:S(2)}, u32[]{:S(2)}) %collective-permute-start.20) | collective-permute-done | bytes 716832 | tf_op jit(solution)/shard_map/ppermute | solution.py:23
  40.4 5.7 %collective-permute-done.5.refs_6_.refs_10_ = bf16[144,840]{1,0:T(8,128)(2,1)S(1)} collective-permute-done((bf16[144,840]{1,0:T(8,128)(2,1)S(1)}, bf16[144,840]{1,0:T(8,128)(2,1)S(1)}, u32[]{:S(2)}, u32[]{:S(2)}) %collective-permute-start.5) | collective-permute-done | bytes 241952 | tf_op jit(solution)/shard_map/ppermute | solution.py:91
  57.6 5.8 %collective-permute-done.24 = bf16[40,1120]{1,0:T(8,128)(2,1)S(1)} collective-permute-done((bf16[40,1120]{1,0:T(8,128)(2,1)S(1)}, bf16[40,1120]{1,0:T(8,128)(2,1)S(1)}, u32[]{:S(2)}, u32[]{:S(2)}) %collective-permute-start.24) | collective-permute-done | bytes 89632 | tf_op jit(solution)/shard_map/ppermute | solution.py:80
  66.9 6.9 %collective-permute-done.19.refs_13_ = bf16[144,840]{1,0:T(8,128)(2,1)S(1)} collective-permute-done((bf16[144,840]{1,0:T(8,128)(2,1)S(1)}, bf16[144,840]{1,0:T(8,128)(2,1)S(1)}, u32[]{:S(2)}, u32[]{:S(2)}) %collective-permute-start.19) | collective-permute-done | bytes 241952 | tf_op jit(solution)/shard_map/ppermute | solution.py:23
  75.5 8.0 %attend_far.1 = (bf16[1120,840]{1,0:T(8,128)(2,1)S(1)}, bf16[2,320,840]{2,1,0:T(8,128)(2,1)S(1)}, bf16[2,320,280]{2,1,0:T(8,128)(2,1)S(1)}, f32[8,128]{1,0:T(8,128)S(1)}) custom-call(s32[1]{0:T(128)} %bitcast.refs_0_, s32[1]{0:T(128)} %bitcast.1.refs_1_.refs_2_.refs_0_, s32[1]{0:T(128)} %collective-permute-done.15.refs_2_.refs_0_, ...), custom_call_target="tpu_custom_call" | custom-call | flops 1728512000 | bytes 7398720 | tf_op jit(solution)/shard_map/attend_far/pallas_call | solution.py:58
  89.3 4.4 %collective-permute-done.31.refs_10_ = bf16[3,40,1120]{2,1,0:T(8,128)(2,1)S(1)} collective-permute-done((bf16[3,40,1120]{2,1,0:T(8,128)(2,1)S(1)}, bf16[3,40,1120]{2,1,0:T(8,128)(2,1)S(1)}, u32[]{:S(2)}, u32[]{:S(2)}) %collective-permute-start.31) | collective-permute-done | bytes 268832 | tf_op jit(solution)/shard_map/ppermute | solution.py:23
  94.4 9.2 %collective-permute-done.28.refs_7_ = bf16[3,40,1120]{2,1,0:T(8,128)(2,1)S(1)} collective-permute-done((bf16[3,40,1120]{2,1,0:T(8,128)(2,1)S(1)}, bf16[3,40,1120]{2,1,0:T(8,128)(2,1)S(1)}, u32[]{:S(2)}, u32[]{:S(2)}) %collective-permute-start.28) | collective-permute-done | bytes 268832 | tf_op jit(solution)/shard_map/ppermute | solution.py:23
  105.6 7.1 %attend_near.1 = (bf16[2,320,840]{2,1,0:T(8,128)(2,1)S(1)}, bf16[320,280]{1,0:T(8,128)(2,1)S(1)}, bf16[320,280]{1,0:T(8,128)(2,1)S(1)}, f32[8,128]{1,0:T(8,128)S(1)}) custom-call(s32[1]{0:T(128)S(6)} %copy.37.refs_0_, s32[1]{0:T(128)} %collective-permute-done.33.refs_1_, bf16[1120,840]{1,0:T(8,128)(2,1)S(1)} %get-tuple-element.159.refs_2_, ...), custom_call_target="tpu_custom_call" | custom-call | flops 1728512000 | bytes 4751040 | tf_op jit(solution)/shard_map/attend_near/pallas_call | solution.py:58
  113.1 4.2 collective-permute-done.32.refs_11_
  126.7 15.2 %collective-permute-done.14.refs_6_.refs_10_ = bf16[280,1120]{1,0:T(8,128)(2,1)S(1)} collective-permute-done((bf16[280,1120]{1,0:T(8,128)(2,1)S(1)}, bf16[280,1120]{1,0:T(8,128)(2,1)S(1)}, u32[]{:S(2)}, u32[]{:S(2)}) %collective-permute-start.14) | collective-permute-done | bytes 627232 | tf_op jit(solution)/shard_map/ppermute | solution.py:91
  145.3 15.3 %collective-permute-done.35.refs_12_ = bf16[280,1120]{1,0:T(8,128)(2,1)S(1)} collective-permute-done((bf16[280,1120]{1,0:T(8,128)(2,1)S(1)}, bf16[280,1120]{1,0:T(8,128)(2,1)S(1)}, u32[]{:S(2)}, u32[]{:S(2)}) %collective-permute-start.35) | collective-permute-done | bytes 627232 | tf_op jit(solution)/shard_map/ppermute | solution.py:23
  160.6 13.1 %collective-permute-done.39.refs_13_ = bf16[280,1120]{1,0:T(8,128)(2,1)S(1)} collective-permute-done((bf16[280,1120]{1,0:T(8,128)(2,1)S(1)}, bf16[280,1120]{1,0:T(8,128)(2,1)S(1)}, u32[]{:S(2)}, u32[]{:S(2)}) %collective-permute-start.39) | collective-permute-done | bytes 627232 | tf_op jit(solution)/shard_map/ppermute | solution.py:23
  174.8 22.3 %feed.1 = (bf16[1280,1120]{1,0:T(8,128)(2,1)}, bf16[1280,1120]{1,0:T(8,128)(2,1)}, f32[1,1120]{1,0:T(1,128)S(1)}, bf16[1120,1120]{1,0:T(8,128)(2,1)}, f32[320,11...) custom-call(s32[1]{0:T(128)} %bitcast.refs_0_, ...), custom_call_target="tpu_custom_call" | custom-call | flops 9633792000 | bytes 27068160 | tf_op jit(solution)/shard_map/feed/pallas_call | solution.py:58
  212.9 5.5 %feed_out.1 = (f32[320,1120]{1,0:T(8,128)S(1)}, bf16[2,320,1120]{2,1,0:T(8,128)(2,1)}, f32[320,1120]{1,0:T(8,128)S(1)}, f32[8,128]{1,0:T(8,128)S(1)}) custom-call(bf16[1280,1120]{1,0:T(8,128)(2,1)S(1)} %copy-done.7, bf16[1120,1120]{1,0:T(8,128)(2,1)S(1)} %copy-done.100, f32[8,128]{1,0:T(8,128)S(1)} %get-tuple-element.184.refs_2_), custom_call_target="tpu_custom_call" | custom-call | flops 3211264000 | bytes 9676800 | tf_op jit(solution)/shard_map/feed_out/pallas_call | solution.py:58
  219.5 6.0 %collective-permute-done.48.refs_3_ = bf16[320,1120]{1,0:T(8,128)(2,1)S(1)} collective-permute-done((bf16[320,1120]{1,0:T(8,128)(2,1)S(1)}, bf16[320,1120]{1,0:T(8,128)(2,1)S(1)}, u32[]{:S(2)}, u32[]{:S(2)}) %collective-permute-start.48) | collective-permute-done | bytes 716832 | tf_op jit(solution)/shard_map/ppermute | solution.py:23
  233.1 6.3 %collective-permute-done.50.refs_6_ = bf16[4,280,560]{2,1,0:T(8,128)(2,1)S(1)} collective-permute-done((bf16[4,280,560]{2,1,0:T(8,128)(2,1)S(1)}, bf16[4,280,560]{2,1,0:T(8,128)(2,1)S(1)}, u32[]{:S(2)}, u32[]{:S(2)}) %collective-permute-start.50) | collective-permute-done | bytes 1254432 | tf_op jit(solution)/shard_map/ppermute | solution.py:23
  243.7 4.3 %all-to-all-start = ((bf16[4,280,560]{2,1,0:T(8,128)(2,1)}), bf16[4,280,560]{2,1,0:T(8,128)(2,1)}, u32[]{:S(2)}, u32[]{:S(2)}) async-start(bf16[4,280,560]{2,1,0:T(8,128)(2,1)} %copy-done.23), calls=%async_computation | async-start | bytes 2867200 | tf_op jit(solution)/shard_map/all_to_all | solution.py:84
  254.2 9.8 %collective-permute-done.53.refs_3_ = bf16[2,320,280]{2,1,0:T(8,128)(2,1)S(1)} collective-permute-done((bf16[2,320,280]{2,1,0:T(8,128)(2,1)}, bf16[2,320,280]{2,1,0:T(8,128)(2,1)S(1)}, u32[]{:S(2)}, u32[]{:S(2)}) %collective-permute-start.53) | collective-permute-done | bytes 358432 | tf_op jit(solution)/shard_map/ppermute | solution.py:23
  266.0 10.1 %attend_back_near.1 = (bf16[2,320,840]{2,1,0:T(8,128)(2,1)S(1)}, f32[8,128]{1,0:T(8,128)S(1)}) custom-call(s32[1]{0:T(128)S(6)} %copy.37.refs_0_, s32[1]{0:T(128)} %collective-permute-done.33.refs_1_, bf16[2,320,840]{2,1,0:T(8,128)(2,1)S(1)} %copy-done.93, bf16[320,280]{1,0:T(8,128)(2,1)S(1)} %copy-done.86, ...), custom_call_target="tpu_custom_call" | custom-call | flops 2621440000 | bytes 2508800 | tf_op jit(solution)/shard_map/attend_back_near/pallas_call | solution.py:58
  277.1 4.2 collective-permute-done.56.refs_6_
  287.0 10.4 %attend_back_far.1 = (bf16[2,320,840]{2,1,0:T(8,128)(2,1)S(1)}, f32[8,128]{1,0:T(8,128)S(1)}) custom-call(s32[1]{0:T(128)} %collective-permute-done.15.refs_2_.refs_0_, s32[1]{0:T(128)} %collective-permute-done.16.refs_3_.refs_1_, bf16[2,320,840]{2,1,0:T(8,128)(2,1)S(1)} %copy-done.91, bf16[2,320,280]{2,1,0:T(8,128)(2,1)S(1)} %collective-permute-done.53.refs_3_, ...), custom_call_target="tpu_custom_call" | custom-call | flops 2621440000 | bytes 2688000 | tf_op jit(solution)/shard_map/attend_back_far/pallas_call | solution.py:58
  298.5 5.0 %all-to-all-start.1 = ((bf16[4,280,560]{2,1,0:T(8,128)(2,1)}), bf16[4,280,560]{2,1,0:T(8,128)(2,1)}, u32[]{:S(2)}, u32[]{:S(2)}) async-start(bf16[4,280,560]{2,1,0:T(8,128)(2,1)} %copy-done.24), calls=%async_computation.1 | async-start | bytes 2867200 | tf_op jit(solution)/shard_map/all_to_all | solution.py:84
  310.4 4.5 %qkv_grad.1 = (bf16[4,144,840]{2,1,0:T(8,128)(2,1)}, bf16[4,144,840]{2,1,0:T(8,128)(2,1)S(1)}, f32[1,840]{1,0:T(1,128)S(1)}, f32[8,128]{1,0:T(8,128)S(1)}) custom-call(s32[1]{0:T(128)} %bitcast.1.refs_1_.refs_2_.refs_0_, bf16[320,1120]{1,0:T(8,128)(2,1)S(1)} %copy-done.71, bf16[320,1120]{1,0:T(8,128)(2,1)S(1)} %copy-done.73, ...), custom_call_target="tpu_custom_call" | custom-call | flops 2408448000 | bytes 6956320 | tf_op jit(solution)/shard_map/qkv_grad/pallas_call | solution.py:58
  314.9 3.7 one_back.1
  322.4 17.8 %collective-permute-done.51.refs_3_ = bf16[320,1120]{1,0:T(8,128)(2,1)S(1)} collective-permute-done((bf16[320,1120]{1,0:T(8,128)(2,1)S(1)}, bf16[320,1120]{1,0:T(8,128)(2,1)S(1)}, u32[]{:S(2)}, u32[]{:S(2)}) %collective-permute-start.51) | collective-permute-done | bytes 716832 | tf_op jit(solution)/shard_map/ppermute | solution.py:23
  350.5 5.2 %all-to-all-start.3 = ((bf16[4,144,840]{2,1,0:T(8,128)(2,1)}), bf16[4,144,840]{2,1,0:T(8,128)(2,1)S(1)}, u32[]{:S(2)}, u32[]{:S(2)}) async-start(bf16[4,144,840]{2,1,0:T(8,128)(2,1)} %copy-done.25), calls=%async_computation.3 | async-start | bytes 2064384 | tf_op jit(solution)/shard_map/all_to_all | solution.py:84
  357.8 17.2 %collective-permute-done.65.refs_3_ = bf16[2,280,560]{2,1,0:T(8,128)(2,1)S(1)} collective-permute-done((bf16[2,280,560]{2,1,0:T(8,128)(2,1)}, bf16[2,280,560]{2,1,0:T(8,128)(2,1)S(1)}, u32[]{:S(2)}, u32[]{:S(2)}) %collective-permute-start.65) | collective-permute-done | bytes 627232 | tf_op jit(solution)/shard_map/ppermute | solution.py:23
  375.2 10.1 %collective-permute-done.59.refs_1_ = bf16[1,140,1120]{2,1,0:T(8,128)(2,1)S(1)} collective-permute-done((bf16[1,140,1120]{2,1,0:T(8,128)(2,1)}, bf16[1,140,1120]{2,1,0:T(8,128)(2,1)S(1)}, u32[]{:S(2)}, u32[]{:S(2)}) %collective-permute-start.59) | collective-permute-done | bytes 313632 | tf_op jit(solution)/shard_map/ppermute | solution.py:23
  396.5 10.4 %all_to_all.25 = f32[4,12,280]{2,1,0:T(8,128)S(1)} all-to-all(f32[4,12,280]{2,1,0:T(8,128)S(1)} %get-tuple-element.247), channel_id=1, replica_groups=mesh['o'=1,'y'=2,'x'=2,'c'=2,'z'=4] {'z'}, dimensions={0} | all-to-all | bytes 107520 | tf_op jit(solution)/shard_map/all_to_all | solution.py:84
  406.9 3.5 all-to-all-start.4
  (394 shorter events, 156.2 us)
Async XLA Ops:
  26.1 28.7 %collective-permute-start.34 = (bf16[320,1120]{1,0:T(8,128)(2,1)S(1)}, bf16[320,1120]{1,0:T(8,128)(2,1)S(1)}, u32[]{:S(2)}, u32[]{:S(2)}) collective-permute-start(bf16[320,1120]{1,0:T(8,128)(2,1)S(1)} %get-tuple-element.151.refs_3_.refs_1_), channel_id=1, source_target_pairs={{0,4},{4,0},{1,5},{5,1},{2,6},{6,2},{3,7},{7,3},{8,12},{12,8},{9,1... | collective-permute-start | bytes 2150408 | tf_op jit(solution)/shard_map/ppermute | solution.py:23
  35.6 39.0 %collective-permute-start.21 = (bf16[320,1120]{1,0:T(8,128)(2,1)S(1)}, bf16[320,1120]{1,0:T(8,128)(2,1)S(1)}, u32[]{:S(2)}, u32[]{:S(2)}) collective-permute-start(bf16[320,1120]{1,0:T(8,128)(2,1)S(1)} %collective-permute-done.20.refs_2_.refs_14_.refs_3_), channel_id=1, source_target_pairs={{0,4},{4,0},{1,5},{5,1},{2,6},{6,2},{3,7},{7,3},{8,12},{12,8},{9,1... | collective-permute-start | bytes 2150408 | tf_op jit(solution)/shard_map/ppermute | solution.py:23
  56.3 30.9 %collective-permute-start.12 = (bf16[280,1120]{1,0:T(8,128)(2,1)S(1)}, bf16[280,1120]{1,0:T(8,128)(2,1)S(1)}, u32[]{:S(2)}, u32[]{:S(2)}) collective-permute-start(bf16[280,1120]{1,0:T(8,128)(2,1)S(1)} %get-tuple-element.146), channel_id=1, source_target_pairs={{1,0},{2,1},{3,2},{5,4},{6,5},{7,6},{9,8},{10,9},{11,10},{13,12},{... | collective-permute-start | bytes 1881608 | tf_op jit(solution)/shard_map/ppermute | solution.py:91
  63.4 25.1 %collective-permute-start.9 = (bf16[280,1120]{1,0:T(8,128)(2,1)S(1)}, bf16[280,1120]{1,0:T(8,128)(2,1)S(1)}, u32[]{:S(2)}, u32[]{:S(2)}) collective-permute-start(bf16[280,1120]{1,0:T(8,128)(2,1)S(1)} %get-tuple-element.146), channel_id=1, source_target_pairs={{0,1},{1,2},{2,3},{4,5},{5,6},{6,7},{8,9},{9,10},{10,11},{12,13},{... | collective-permute-start | bytes 1881608 | tf_op jit(solution)/shard_map/ppermute | solution.py:90
  83.6 21.5 %collective-permute-start.37 = (bf16[2,320,280]{2,1,0:T(8,128)(2,1)S(1)}, bf16[2,320,280]{2,1,0:T(8,128)(2,1)S(1)}, u32[]{:S(2)}, u32[]{:S(2)}) collective-permute-start(bf16[2,320,280]{2,1,0:T(8,128)(2,1)S(1)} %get-tuple-element.166), channel_id=1, source_target_pairs={{0,8},{8,0},{1,9},{9,1},{2,10},{10,2},{3,11},{11,3},{4,12},{12,4},... | collective-permute-start | bytes 1075208 | tf_op jit(solution)/shard_map/ppermute | solution.py:23
  87.2 30.8 %collective-permute-start.13 = (bf16[280,1120]{1,0:T(8,128)(2,1)S(1)}, bf16[280,1120]{1,0:T(8,128)(2,1)S(1)}, u32[]{:S(2)}, u32[]{:S(2)}) collective-permute-start(bf16[280,1120]{1,0:T(8,128)(2,1)S(1)} %collective-permute-done.12.refs_2_.refs_3_.refs_4_.refs_8_), channel_id=1, source_target_pairs={{1,0},{2,1},{5,4},{6,5},{9,8},{10,9},{13,12},{14,13},{17,16},{18,1... | collective-permute-start | bytes 1881608 | tf_op jit(solution)/shard_map/ppermute | solution.py:91
  88.5 29.6 %collective-permute-start.10 = (bf16[280,1120]{1,0:T(8,128)(2,1)S(1)}, bf16[280,1120]{1,0:T(8,128)(2,1)S(1)}, u32[]{:S(2)}, u32[]{:S(2)}) collective-permute-start(bf16[280,1120]{1,0:T(8,128)(2,1)S(1)} %collective-permute-done.9.refs_1_.refs_5_), channel_id=1, source_target_pairs={{1,2},{2,3},{5,6},{6,7},{9,10},{10,11},{13,14},{14,15},{17,18},{18... | collective-permute-start | bytes 1881608 | tf_op jit(solution)/shard_map/ppermute | solution.py:90
  93.7 31.4 %collective-permute-start.44 = (bf16[320,1120]{1,0:T(8,128)(2,1)S(1)}, bf16[320,1120]{1,0:T(8,128)(2,1)S(1)}, u32[]{:S(2)}, u32[]{:S(2)}) collective-permute-start(bf16[320,1120]{1,0:T(8,128)(2,1)S(1)} %get-tuple-element.173.refs_18_.refs_2_), channel_id=1, source_target_pairs={{0,8},{8,0},{1,9},{9,1},{2,10},{10,2},{3,11},{11,3},{4,12},{12,4},... | collective-permute-start | bytes 2150408 | tf_op jit(solution)/shard_map/ppermute | solution.py:23
  121.8 20.6 %collective-permute-start.41 = (bf16[320,1120]{1,0:T(8,128)(2,1)S(1)}, bf16[320,1120]{1,0:T(8,128)(2,1)S(1)}, u32[]{:S(2)}, u32[]{:S(2)}) collective-permute-start(bf16[320,1120]{1,0:T(8,128)(2,1)S(1)} %get-tuple-element.172.refs_14_.refs_1_), channel_id=1, source_target_pairs={{0,8},{8,0},{1,9},{9,1},{2,10},{10,2},{3,11},{11,3},{4,12},{12,4},... | collective-permute-start | bytes 2150408 | tf_op jit(solution)/shard_map/ppermute | solution.py:23
  123.0 20.2 %collective-permute-start.43 = (bf16[320,1120]{1,0:T(8,128)(2,1)S(1)}, bf16[320,1120]{1,0:T(8,128)(2,1)S(1)}, u32[]{:S(2)}, u32[]{:S(2)}) collective-permute-start(bf16[320,1120]{1,0:T(8,128)(2,1)S(1)} %get-tuple-element.173.refs_18_.refs_2_), channel_id=1, source_target_pairs={{0,4},{4,0},{1,5},{5,1},{2,6},{6,2},{3,7},{7,3},{8,12},{12,8},{9,1... | collective-permute-start | bytes 2150408 | tf_op jit(solution)/shard_map/ppermute | solution.py:23
  123.0 18.8 %collective-permute-start.14 = (bf16[280,1120]{1,0:T(8,128)(2,1)S(1)}, bf16[280,1120]{1,0:T(8,128)(2,1)S(1)}, u32[]{:S(2)}, u32[]{:S(2)}) collective-permute-start(bf16[280,1120]{1,0:T(8,128)(2,1)S(1)} %collective-permute-done.13.refs_4_.refs_5_.refs_9_), channel_id=1, source_target_pairs={{1,0},{5,4},{9,8},{13,12},{17,16},{21,20},{25,24},{29,28}} | collective-permute-start | bytes 1881608 | tf_op jit(solution)/shard_map/ppermute | solution.py:91
  125.1 19.7 %collective-permute-start.22 = (bf16[280,1120]{1,0:T(8,128)(2,1)S(1)}, bf16[280,1120]{1,0:T(8,128)(2,1)S(1)}, u32[]{:S(2)}, u32[]{:S(2)}) collective-permute-start(bf16[280,1120]{1,0:T(8,128)(2,1)S(1)} %get-tuple-element.157), channel_id=1, source_target_pairs={{0,16},{16,0},{1,17},{17,1},{2,18},{18,2},{3,19},{19,3},{4,20},{20... | collective-permute-start | bytes 1881608 | tf_op jit(solution)/shard_map/ppermute | solution.py:23
  141.9 18.7 %collective-permute-start.40 = (bf16[320,1120]{1,0:T(8,128)(2,1)S(1)}, bf16[320,1120]{1,0:T(8,128)(2,1)S(1)}, u32[]{:S(2)}, u32[]{:S(2)}) collective-permute-start(bf16[320,1120]{1,0:T(8,128)(2,1)S(1)} %get-tuple-element.172.refs_14_.refs_1_), channel_id=1, source_target_pairs={{0,4},{4,0},{1,5},{5,1},{2,6},{6,2},{3,7},{7,3},{8,12},{12,8},{9,1... | collective-permute-start | bytes 2150408 | tf_op jit(solution)/shard_map/ppermute | solution.py:23
  142.4 31.3 %collective-permute-start.42 = (bf16[320,1120]{1,0:T(8,128)(2,1)S(1)}, bf16[320,1120]{1,0:T(8,128)(2,1)S(1)}, u32[]{:S(2)}, u32[]{:S(2)}) collective-permute-start(bf16[320,1120]{1,0:T(8,128)(2,1)S(1)} %collective-permute-done.41.refs_16_.refs_3_), channel_id=1, source_target_pairs={{0,4},{4,0},{1,5},{5,1},{2,6},{6,2},{3,7},{7,3},{8,12},{12,8},{9,1... | collective-permute-start | bytes 2150408 | tf_op jit(solution)/shard_map/ppermute | solution.py:23
  144.8 28.9 %collective-permute-start.39 = (bf16[280,1120]{1,0:T(8,128)(2,1)S(1)}, bf16[280,1120]{1,0:T(8,128)(2,1)S(1)}, u32[]{:S(2)}, u32[]{:S(2)}) collective-permute-start(bf16[280,1120]{1,0:T(8,128)(2,1)S(1)} %get-tuple-element.171), channel_id=1, source_target_pairs={{0,16},{16,0},{1,17},{17,1},{2,18},{18,2},{3,19},{19,3},{4,20},{20... | collective-permute-start | bytes 1881608 | tf_op jit(solution)/shard_map/ppermute | solution.py:23
  205.5 33.9 %collective-permute-start.50 = (bf16[4,280,560]{2,1,0:T(8,128)(2,1)S(1)}, bf16[4,280,560]{2,1,0:T(8,128)(2,1)S(1)}, u32[]{:S(2)}, u32[]{:S(2)}) collective-permute-start(bf16[4,280,560]{2,1,0:T(8,128)(2,1)S(1)} %get-tuple-element.198), channel_id=1, source_target_pairs={{0,16},{16,0},{1,17},{17,1},{2,18},{18,2},{3,19},{19,3},{4,20},{20... | collective-permute-start | bytes 3763208 | tf_op jit(solution)/shard_map/ppermute | solution.py:23
  206.8 18.7 %collective-permute-start.48 = (bf16[320,1120]{1,0:T(8,128)(2,1)S(1)}, bf16[320,1120]{1,0:T(8,128)(2,1)S(1)}, u32[]{:S(2)}, u32[]{:S(2)}) collective-permute-start(bf16[320,1120]{1,0:T(8,128)(2,1)S(1)} %get-tuple-element.189), channel_id=1, source_target_pairs={{0,8},{8,0},{1,9},{9,1},{2,10},{10,2},{3,11},{11,3},{4,12},{12,4},... | collective-permute-start | bytes 2150408 | tf_op jit(solution)/shard_map/ppermute | solution.py:23
  232.6 17.9 %collective-permute-start.49 = (bf16[4,140,1120]{2,0,1:T(4,128)(2,1)}, bf16[4,140,1120]{2,0,1:T(4,128)(2,1)}, u32[]{:S(2)}, u32[]{:S(2)}) collective-permute-start(bf16[4,140,1120]{2,0,1:T(4,128)(2,1)} %copy.32), channel_id=1, source_target_pairs={{0,4},{4,0},{1,5},{5,1},{2,6},{6,2},{3,7},{7,3},{8,12},{12,8},{9,1... | collective-permute-start | bytes 3763208 | tf_op jit(solution)/shard_map/ppermute | solution.py:23
  232.6 31.6 %collective-permute-start.47 = (bf16[2,320,1120]{2,1,0:T(8,128)(2,1)}, bf16[2,320,1120]{2,1,0:T(8,128)(2,1)}, u32[]{:S(2)}, u32[]{:S(2)}) collective-permute-start(bf16[2,320,1120]{2,1,0:T(8,128)(2,1)} %get-tuple-element.186), channel_id=1, source_target_pairs={{0,4},{4,0},{1,5},{5,1},{2,6},{6,2},{3,7},{7,3},{8,12},{12,8},{9,1... | collective-permute-start | bytes 4300808 | tf_op jit(solution)/shard_map/ppermute | solution.py:23
  243.7 54.8 %all-to-all-start = ((bf16[4,280,560]{2,1,0:T(8,128)(2,1)}), bf16[4,280,560]{2,1,0:T(8,128)(2,1)}, u32[]{:S(2)}, u32[]{:S(2)}) async-start(bf16[4,280,560]{2,1,0:T(8,128)(2,1)} %copy-done.23), calls=%async_computation | async-start | bytes 2867200 | tf_op jit(solution)/shard_map/all_to_all | solution.py:84
  248.1 33.3 %collective-permute-start.56 = (bf16[4,280,560]{2,1,0:T(8,128)(2,1)}, bf16[4,280,560]{2,1,0:T(8,128)(2,1)S(1)}, u32[]{:S(2)}, u32[]{:S(2)}) collective-permute-start(bf16[4,280,560]{2,1,0:T(8,128)(2,1)} %copy-done.69), channel_id=1, source_target_pairs={{0,16},{16,0},{1,17},{17,1},{2,18},{18,2},{3,19},{19,3},{4,20},{20... | collective-permute-start | bytes 3763208 | tf_op jit(solution)/shard_map/ppermute | solution.py:23
  252.9 31.5 %collective-permute-start.55 = (bf16[2,140,1120]{2,0,1:T(2,128)(2,1)S(1)}, bf16[2,140,1120]{2,0,1:T(2,128)(2,1)S(1)}, u32[]{:S(2)}, u32[]{:S(2)}) collective-permute-start(bf16[2,140,1120]{2,0,1:T(2,128)(2,1)S(1)} %copy.34), channel_id=1, source_target_pairs={{0,8},{8,0},{1,9},{9,1},{2,10},{10,2},{3,11},{11,3},{4,12},{12,4},... | collective-permute-start | bytes 1881608 | tf_op jit(solution)/shard_map/ppermute | solution.py:23
  264.1 23.0 %collective-permute-start.54 = (bf16[320,280]{1,0:T(8,128)(2,1)S(1)}, bf16[320,280]{1,0:T(8,128)(2,1)S(1)}, u32[]{:S(2)}, u32[]{:S(2)}) collective-permute-start(bf16[320,280]{1,0:T(8,128)(2,1)S(1)} %slice_bitcast_fusion), channel_id=1, source_target_pairs={{0,4},{4,0},{1,5},{5,1},{2,6},{6,2},{3,7},{7,3},{8,12},{12,8},{9,1... | collective-permute-start | bytes 537608 | tf_op jit(solution)/shard_map/ppermute | solution.py:23
  298.5 46.6 %all-to-all-start.1 = ((bf16[4,280,560]{2,1,0:T(8,128)(2,1)}), bf16[4,280,560]{2,1,0:T(8,128)(2,1)}, u32[]{:S(2)}, u32[]{:S(2)}) async-start(bf16[4,280,560]{2,1,0:T(8,128)(2,1)} %copy-done.24), calls=%async_computation.1 | async-start | bytes 2867200 | tf_op jit(solution)/shard_map/all_to_all | solution.py:84
  319.7 23.2 %collective-permute-start.57 = (bf16[2,320,1120]{2,1,0:T(8,128)(2,1)S(1)}, bf16[2,320,1120]{2,1,0:T(8,128)(2,1)S(1)}, u32[]{:S(2)}, u32[]{:S(2)}) collective-permute-start(bf16[2,320,1120]{2,1,0:T(8,128)(2,1)S(1)} %get-tuple-element.222), channel_id=1, source_target_pairs={{0,4},{4,0},{1,5},{5,1},{2,6},{6,2},{3,7},{7,3},{8,12},{12,8},{9,1... | collective-permute-start | bytes 4300808 | tf_op jit(solution)/shard_map/ppermute | solution.py:23
  319.7 27.5 %collective-permute-start.60 = (bf16[4,144,840]{2,1,0:T(8,128)(2,1)}, bf16[4,144,840]{2,1,0:T(8,128)(2,1)}, u32[]{:S(2)}, u32[]{:S(2)}) collective-permute-start(bf16[4,144,840]{2,1,0:T(8,128)(2,1)} %get-tuple-element.230), channel_id=1, source_target_pairs={{0,16},{16,0},{1,17},{17,1},{2,18},{18,2},{3,19},{19,3},{4,20},{20... | collective-permute-start | bytes 2903048 | tf_op jit(solution)/shard_map/ppermute | solution.py:23
  321.7 18.6 %collective-permute-start.51 = (bf16[320,1120]{1,0:T(8,128)(2,1)S(1)}, bf16[320,1120]{1,0:T(8,128)(2,1)S(1)}, u32[]{:S(2)}, u32[]{:S(2)}) collective-permute-start(bf16[320,1120]{1,0:T(8,128)(2,1)S(1)} %copy-done.79), channel_id=1, source_target_pairs={{0,8},{8,0},{1,9},{9,1},{2,10},{10,2},{3,11},{11,3},{4,12},{12,4},... | collective-permute-start | bytes 2150408 | tf_op jit(solution)/shard_map/ppermute | solution.py:23
  350.5 44.9 %all-to-all-start.3 = ((bf16[4,144,840]{2,1,0:T(8,128)(2,1)}), bf16[4,144,840]{2,1,0:T(8,128)(2,1)S(1)}, u32[]{:S(2)}, u32[]{:S(2)}) async-start(bf16[4,144,840]{2,1,0:T(8,128)(2,1)} %copy-done.25), calls=%async_computation.3 | async-start | bytes 2064384 | tf_op jit(solution)/shard_map/all_to_all | solution.py:84
  355.7 19.2 %collective-permute-start.65 = (bf16[2,280,560]{2,1,0:T(8,128)(2,1)}, bf16[2,280,560]{2,1,0:T(8,128)(2,1)S(1)}, u32[]{:S(2)}, u32[]{:S(2)}) collective-permute-start(bf16[2,280,560]{2,1,0:T(8,128)(2,1)} %copy-done.53), channel_id=1, source_target_pairs={{0,8},{8,0},{1,9},{9,1},{2,10},{10,2},{3,11},{11,3},{4,12},{12,4},... | collective-permute-start | bytes 1881608 | tf_op jit(solution)/shard_map/ppermute | solution.py:23
  356.5 32.4 %collective-permute-start.58 = (bf16[320,1120]{1,0:T(8,128)(2,1)}, bf16[320,1120]{1,0:T(8,128)(2,1)S(1)}, u32[]{:S(2)}, u32[]{:S(2)}) collective-permute-start(bf16[320,1120]{1,0:T(8,128)(2,1)} %copy-done.80), channel_id=1, source_target_pairs={{0,8},{8,0},{1,9},{9,1},{2,10},{10,2},{3,11},{11,3},{4,12},{12,4},... | collective-permute-start | bytes 2150408 | tf_op jit(solution)/shard_map/ppermute | solution.py:23
  357.8 36.5 %collective-permute-start.64 = (bf16[2,280,560]{2,1,0:T(8,128)(2,1)}, bf16[2,280,560]{2,1,0:T(8,128)(2,1)S(1)}, u32[]{:S(2)}, u32[]{:S(2)}) collective-permute-start(bf16[2,280,560]{2,1,0:T(8,128)(2,1)} %copy-done.53), channel_id=1, source_target_pairs={{0,4},{4,0},{1,5},{5,1},{2,6},{6,2},{3,7},{7,3},{8,12},{12,8},{9,1... | collective-permute-start | bytes 1881608 | tf_op jit(solution)/shard_map/ppermute | solution.py:23
  374.9 19.4 %collective-permute-start.66 = (bf16[2,280,560]{2,1,0:T(8,128)(2,1)S(1)}, bf16[2,280,560]{2,1,0:T(8,128)(2,1)S(1)}, u32[]{:S(2)}, u32[]{:S(2)}) collective-permute-start(bf16[2,280,560]{2,1,0:T(8,128)(2,1)S(1)} %collective-permute-done.65.refs_3_), channel_id=1, source_target_pairs={{0,4},{4,0},{1,5},{5,1},{2,6},{6,2},{3,7},{7,3},{8,12},{12,8},{9,1... | collective-permute-start | bytes 1881608 | tf_op jit(solution)/shard_map/ppermute | solution.py:23
  (147 other events, 1655.7 us)
